TPU v7x, 32 devices: a whole 2x2x4 slice. The times are simulated.
32 devices in a mesh: row: 8 (over y, x, core), col: 4 (over z).
Axes of the slice: x: 2, y: 2, z: 4, core: 2. Of those that a mesh axis runs over, the one named last changes fastest.
Arguments:
- activations: bfloat16 [8192, 2048], P('col', 'row'), may hold values from -6 to 6
- document_ids: int32 [8192], P('col'), may hold values from 0 to 15, never falling along the last dimension, each value on 1 to 2048 neighbouring positions
- attention_gain: float32 [2048], P('row'), may hold values from 0.5 to 1.5
- attention_shift: float32 [2048], P('row'), may hold values from -1.75 to 1.75
- feedforward_gain: float32 [2048], P('row'), may hold values from 0.5 to 1.5
- feedforward_shift: float32 [2048], P('row'), may hold values from -1.75 to 1.75
- query_key_value: float32 [2048, 16, 384], P('col', 'row'), may hold values from -1 to 1
- query_key_value_bias: float32 [16, 384], P('row'), may hold values from -3 to 3
- output_weight: float32 [2048, 2048], P('row', 'col'), may hold values from -0.5 to 0.5
- output_bias: float32 [2048], P('row'), may hold values from -1.75 to 1.75
- up_weight: float32 [2048, 8192], P('col', 'row'), may hold values from -1 to 1
- up_bias: float32 [8192], P('row'), may hold values from -3 to 3
- down_weight: float32 [8192, 2048], P('row', 'col'), may hold values from -0.0625 to 0.0625
- down_bias: float32 [2048], P('row'), may hold values from -1.75 to 1.75
- out_grad: bfloat16 [8192, 2048], P('col', 'row'), may hold values from -6 to 6
Outputs:
- layer_out: float32 [8192, 2048], P('col', 'row')
- activations_grad: float32 [8192, 2048], P('col', 'row')
- attention_gain_grad: float32 [2048], P('row')
- attention_shift_grad: float32 [2048], P('row')
- feedforward_gain_grad: float32 [2048], P('row')
- feedforward_shift_grad: float32 [2048], P('row')
- query_key_value_grad: float32 [2048, 16, 384], P('col', 'row')
- query_key_value_bias_grad: float32 [16, 384], P('row')
- output_weight_grad: float32 [2048, 2048], P('row', 'col')
- output_bias_grad: float32 [2048], P('row')
- up_weight_grad: float32 [2048, 8192], P('col', 'row')
- up_bias_grad: float32 [8192], P('row')
- down_weight_grad: float32 [8192, 2048], P('row', 'col')
- down_bias_grad: float32 [2048], P('row')
Inputs may be any that keep to these rules, and one draw needn't show every extreme that they name: `document_ids`: ids never fall from one token to the next; attention stays inside a packed row of 2048 tokens.
All inputs are finite; a program needn't handle non-finite values.
Results may differ from a plain program's by a relative error of at most 0.012.
The roundings to bfloat16 on the way count: a program that leaves them out, or rounds other values in their place, can miss the bound.
Values may be sent and summed in bfloat16 or wider, within the bound.
No kernel may reach another device: no remote copies, remote signals or barrier semaphores. Data moves between devices by JAX's collectives and lax.ppermute only.
A program may use at most 256 MiB of HBM per device.

v0:
```python
import functools

import jax
import jax.numpy as jnp
from jax import lax
from jax.experimental import pallas as pl
from jax.experimental.pallas import tpu as pltpu
from jax.sharding import PartitionSpec as P

D = 2048
HEAD_DIM = 128
ROTARY = 32
LENGTH = 2048

EPSILON = 1e-05
MASKED = -1e30
ROPE_BASE = 10000.0
BF = jnp.bfloat16
F32 = jnp.float32
LAST = (((1,), (1,)), ((), ()))
FIRST = (((0,), (0,)), ((), ()))
TILE = 256
QUERY_BLOCK = KEY_BLOCK = 512
VMEM_LIMIT = 56 * 1024 * 1024
LOG2_E = 1.4426950408889634
SQRT_HALF = 0.7071067811865476
INV_SQRT_2PI = 0.3989422804014327


def after(value, gate):
    return lax.optimization_barrier((value,) + tuple(gate))[0] if gate else value


class RingGather:
    def __init__(self, shard, count):
        self.count, self.arrays = count, [shard]

    def step(self, gate):
        count = self.count
        pairs = [(k, (k + 1) % count) for k in range(count)]
        self.arrays = self.arrays + [lax.ppermute(after(self.arrays[-1], gate), "col", pairs)]
        return self.arrays[-1:]

    def shards(self):
        count = self.count
        return self.arrays, [[(i - j) % count for j in range(count)] for i in range(count)]


class RingScatter:
    def __init__(self, chunks, count):
        self.chunks, self.count = chunks, count
        self.moving, self.done = None, 0

    def step(self, gate):
        self.done += 1
        count = self.count
        sent = after(self.chunks[count - self.done], gate)
        if self.moving is not None:
            sent = (sent.astype(F32) + self.moving.astype(F32)).astype(BF)
        pairs = [(k, (k + 1) % count) for k in range(count)]
        self.sent = sent
        self.moving = lax.ppermute(self.sent, "col", pairs)
        return [self.moving]

    def result(self, gate):
        return after(self.chunks[0], gate) + self.moving.astype(F32)


class LineBoth:
    def __init__(self, shard, place):
        self.shard, self.place = shard, place
        self.upward, self.downward = [shard], [shard]

    def step(self, gate):
        place, done = self.place, len(self.upward)
        up, down = self.upward[-1], self.downward[-1]
        if done == 2:
            up = jnp.where(place == 0, self.chunks[3], up)
            down = jnp.where(place == 3, self.chunks[1], down)
        elif done == 3:
            up = jnp.where(place == 2, up, self.add(2, up))
            down = jnp.where(place == 1, down, self.add(2, down))
        elif done == 4:
            up, down = self.add(1, up), self.add(3, down)
        up, down = after(up, gate), after(down, gate)
        self.upward.append(lax.ppermute(up, "col", [(0, 1), (1, 2), (2, 3)]))
        self.downward.append(lax.ppermute(down, "col", [(3, 2), (2, 1), (1, 0)]))
        return [self.upward[-1], self.downward[-1]]

    def add(self, at, array):
        return (self.chunks[at].astype(F32) + array.astype(F32)).astype(BF)

    def shards(self):
        table = [[0 if j == i else i - j if j < i else 3 + j - i for j in range(4)] for i in range(4)]
        return self.upward[:4] + self.downward[1:4], table

    def result(self, gate):
        return after(self.chunks[0], gate) + (self.upward[4].astype(F32) + self.downward[4].astype(F32))


class RowScatter:
    KEPT, SENT = [0, 2, 4, 6], [1, 3, 5, 7]

    def __init__(self, kept, sent):
        self.kept, self.sent, self.done = kept, sent, 0
        self.width, self.parts = kept.shape[1] // 4, []

    def send(self, array, mask, gate):
        self.parts.append(after(array, gate))
        return lax.ppermute(self.parts[-1], "row", [(k, k ^ mask) for k in range(8)])

    def piece(self, at):
        columns = slice(at * self.width, (at + 1) * self.width)
        return self.kept[:, columns].astype(F32) + self.core[:, columns].astype(F32)

    def step(self, gate):
        self.done += 1
        half = self.kept.shape[0] // 2
        if self.done == 1:
            self.core = self.send(self.sent, 1, gate)
            return [self.core]
        if self.done == 2:
            far = self.piece(3).astype(BF)
            self.from_x = self.send(far[:half], 2, gate)
            self.from_y = self.send(far[half:], 4, gate)
        else:
            empty = jnp.zeros_like(self.from_x, F32)
            from_x, from_y = self.from_x.astype(F32), self.from_y.astype(F32)
            for_x = self.piece(1) + jnp.concatenate([empty, from_y])
            for_y = self.piece(2) + jnp.concatenate([from_x, empty])
            self.from_x = self.send(for_x.astype(BF), 2, gate)
            self.from_y = self.send(for_y.astype(BF), 4, gate)
        return [self.from_x, self.from_y]

    def result(self):
        return self.piece(0) + self.from_x.astype(F32) + self.from_y.astype(F32)


def pair_sum(value, axis, count, masks, gate):
    for mask in masks:
        value = value + pair_exchange(value, axis, count, mask, gate)
    return value


def pair_exchange(value, axis, count, mask, gate):
    return lax.ppermute(after(value, gate), axis, [(k, k ^ mask) for k in range(count)])


def pair_scatter(value, axis, count, place):
    mask = count // 2
    while mask:
        upper = lax.rem(place // mask, 2) == 1
        low, high = value[:mask], value[mask:]
        kept, sent = jnp.where(upper, high, low), jnp.where(upper, low, high)
        value = kept + lax.ppermute(sent, axis, [(k, k ^ mask) for k in range(count)])
        mask //= 2
    return value[0]


def load_shards(refs, table, whole, sems, dim, columns=None):
    if columns is not None:
        refs = [ref.at[:, columns] for ref in refs]
    count = len(table)
    extent = refs[0].shape[dim]
    place = lax.axis_index("col")

    def spot(j):
        at = pl.ds(j * extent, extent)
        return whole.at[at, :] if dim == 0 else whole.at[:, at]

    for i in range(count):

        @pl.when(place == i)
        def _():
            for j in range(count):
                pltpu.make_async_copy(refs[table[i][j]], spot(j), sems.at[j]).start()

    for j in range(count):
        pltpu.make_async_copy(refs[0], spot(j), sems.at[j]).wait()


def normalize(tile):
    values = tile.astype(F32)
    centered = values - jnp.mean(values, axis=1, keepdims=True)
    inverse_scale = lax.rsqrt(jnp.mean(centered * centered, axis=1, keepdims=True) + EPSILON)
    return centered * inverse_scale, inverse_scale


def norm_kernel(act, params, first_out, second_out):
    normed, _ = normalize(act[...])
    first_out[...] = (normed * params[0:1, :] + params[1:2, :]).astype(BF)
    second_out[...] = (normed * params[2:3, :] + params[3:4, :]).astype(BF)


def up_kernel(table, *refs):
    norm, bias, *shards = refs[:-4]
    hidden_out, slope_out, whole, sems = refs[-4:]

    @pl.when(pl.program_id(0) == 0)
    def _():
        load_shards(shards, table, whole, sems, 0)

    lin = jnp.dot(norm[...], whole[...], preferred_element_type=F32) + bias[...]
    cdf = 0.5 + 0.5 * lax.erf(lin * SQRT_HALF)
    hidden_out[...] = (lin * cdf).astype(BF)
    slope_out[...] = cdf + lin * (INV_SQRT_2PI * jnp.exp(-0.5 * lin * lin))


def turn(values, tables, sign):
    cosine, left, right = tables
    half = ROTARY // 2
    turned = left * pltpu.roll(values, HEAD_DIM - half, 1) + right * pltpu.roll(values, half, 1)
    return values * cosine + sign * turned


def project_kernel(table, heads, *refs):
    norm, bias, cosine, left, right, *shards = refs[:-3]
    out, whole, sems = refs[-3:]

    @pl.when(pl.program_id(0) == 0)
    def _():
        load_shards(shards, table, whole, sems, 0, pl.ds(0, whole.shape[1]))

    lin = jnp.dot(norm[...], whole[...], preferred_element_type=F32) + bias[...]
    tables = cosine[...], left[...], right[...]
    for head in range(heads):
        for part in range(3):
            at = slice((head * 3 + part) * HEAD_DIM, (head * 3 + part + 1) * HEAD_DIM)
            piece = lin[:, at]
            out[:, at] = (turn(piece, tables, 1.0) if part < 2 else piece).astype(BF)


def attended_grad_kernel(table, *refs):
    grad, *shards = refs[:-3]
    out, whole, sems = refs[-3:]

    @pl.when(pl.program_id(0) == 0)
    def _():
        columns = pl.ds(shards[0].shape[1] - whole.shape[1], whole.shape[1])
        load_shards(shards, table, whole, sems, 0, columns)

    out[...] = jnp.dot(grad[...], whole[...], preferred_element_type=F32).astype(BF)


def head_columns(head, part):
    return slice((3 * head + part) * HEAD_DIM, (3 * head + part + 1) * HEAD_DIM)


def own_columns(head):
    return slice(head * HEAD_DIM, (head + 1) * HEAD_DIM)


def rows_of(block, extent):
    return pl.ds(pl.multiple_of(block * extent, extent), extent)


def allowed_scores(project, start, block, at, head, masked):
    rows, keys = rows_of(block, QUERY_BLOCK), rows_of(at, KEY_BLOCK)
    scores = lax.dot_general(
        project[keys, head_columns(head, 1)],
        project[rows, head_columns(head, 0)],
        LAST,
        preferred_element_type=F32,
    ) * (HEAD_DIM**-0.5 * LOG2_E)
    if not masked:
        return scores
    place = block * QUERY_BLOCK + lax.broadcasted_iota(jnp.int32, (1, QUERY_BLOCK), 1)
    key_place = at * KEY_BLOCK + lax.broadcasted_iota(jnp.int32, (KEY_BLOCK, QUERY_BLOCK), 0)
    allowed = (key_place >= start[:, rows]) & (key_place <= place)
    return jnp.where(allowed, scores, MASKED)


def over_keys(low, high, block, step, carry):
    between = jnp.minimum(high[block], block)
    carry = lax.fori_loop(low[block], between, functools.partial(step, True), carry)
    carry = lax.fori_loop(between, block, functools.partial(step, False), carry)
    return step(True, block, carry)


def attention_kernel(low, high, start, project, *refs):
    out, produced_t, log_total, v_t = refs[-4:]
    v_t[...] = project[:, head_columns(0, 2)].T

    def query_block(block, _):
        rows = rows_of(block, QUERY_BLOCK)

        def forward(masked, at, carry):
            largest, total, produced = carry
            scores = allowed_scores(project, start, block, at, 0, masked)
            newest = jnp.maximum(largest, jnp.max(scores, axis=0, keepdims=True))
            shrink = jnp.exp2(largest - newest)
            parts = jnp.exp2(scores - newest)
            total = total * shrink + jnp.sum(parts, axis=0, keepdims=True)
            produced = produced * shrink + jnp.dot(
                v_t[:, rows_of(at, KEY_BLOCK)], parts.astype(BF), preferred_element_type=F32
            )
            return newest, total, produced

        empty = jnp.zeros((1, QUERY_BLOCK), F32)
        wide = jnp.zeros((HEAD_DIM, QUERY_BLOCK), F32)
        largest, total, produced = over_keys(
            low, high, block, forward, (empty + MASKED, empty, wide)
        )
        produced = produced * (1.0 / total)
        out[rows, :] = produced.T.astype(BF)
        produced_t[:, rows] = produced
        log_total[:, rows] = largest + jnp.log2(total)
        return 0

    lax.fori_loop(0, project.shape[0] // QUERY_BLOCK, query_block, 0)


def attention_back_kernel(
    heads,
    low,
    high,
    start,
    cosine,
    left,
    right,
    project,
    grad,
    *refs,
):
    produced_t, log_total = refs[:heads], refs[heads : 2 * heads]
    project_grad, k_t, dk, dv = refs[2 * heads :]
    length = project.shape[0]
    scale = HEAD_DIM**-0.5
    for head in range(heads):
        k_t[head] = project[:, head_columns(head, 1)].T
    dk[...] = jnp.zeros_like(dk)
    dv[...] = jnp.zeros_like(dv)

    def query_block(block, _):
        rows = rows_of(block, QUERY_BLOCK)
        deltas = [
            jnp.sum(
                produced_t[head][:, rows] * grad[rows, own_columns(head)].astype(F32).T,
                axis=0,
                keepdims=True,
            )
            for head in range(heads)
        ]

        def backward(masked, at, query_grads):
            keys, made = rows_of(at, KEY_BLOCK), []
            for head in range(heads):
                scores = allowed_scores(project, start, block, at, head, masked)
                prob_grad = lax.dot_general(
                    project[keys, head_columns(head, 2)],
                    grad[rows, own_columns(head)],
                    LAST,
                    preferred_element_type=F32,
                )
                probs = jnp.exp2(scores - log_total[head][:, rows])
                score_grad = (probs * (prob_grad - deltas[head])).astype(BF)
                dv[head, keys, :] += jnp.dot(
                    probs.astype(BF), grad[rows, own_columns(head)], preferred_element_type=F32
                )
                dk[head, keys, :] += jnp.dot(
                    score_grad, project[rows, head_columns(head, 0)], preferred_element_type=F32
                )
                made.append(
                    query_grads[head]
                    + jnp.dot(k_t[head, :, keys], score_grad, preferred_element_type=F32)
                )
            return tuple(made)

        wide = jnp.zeros((HEAD_DIM, QUERY_BLOCK), F32)
        query_grads = over_keys(low, high, block, backward, (wide,) * heads)
        tables = cosine[rows, :], left[rows, :], right[rows, :]
        for head in range(heads):
            project_grad[rows, head_columns(head, 0)] = turn(
                (query_grads[head] * scale).T, tables, -1.0
            ).astype(BF)
        return 0

    lax.fori_loop(0, length // QUERY_BLOCK, query_block, 0)
    tables = cosine[...], left[...], right[...]
    for head in range(heads):
        project_grad[:, head_columns(head, 1)] = turn(dk[head] * scale, tables, -1.0).astype(BF)
        project_grad[:, head_columns(head, 2)] = dv[head].astype(BF)


def mixed_kernel(pack_count, pack_table, down_table, *refs):
    attended, hidden, *shards = refs[:-5]
    pack_shards, down_shards = shards[:pack_count], shards[pack_count:]
    out, output_whole, down_whole, output_sems, down_sems = refs[-5:]

    @pl.when(pl.program_id(0) == 0)
    def _():
        width = pack_shards[0].shape[1]
        columns = pl.ds(width - output_whole.shape[1], output_whole.shape[1])
        load_shards(pack_shards, pack_table, output_whole, output_sems, 0, columns)
        load_shards(down_shards, down_table, down_whole, down_sems, 0)

    out[...] = (
        lax.dot_general(attended[...], output_whole[...], LAST, preferred_element_type=F32)
        + lax.dot_general(hidden[...], down_whole[...], LAST, preferred_element_type=F32)
    ).astype(BF)


def hidden_grad_kernel(table, *refs):
    grad, slope, *shards = refs[:-3]
    out, whole, sems = refs[-3:]

    @pl.when(pl.program_id(0) == 0)
    def _():
        load_shards(shards, table, whole, sems, 0)

    hidden_grad = jnp.dot(grad[...], whole[...], preferred_element_type=F32)
    out[...] = (hidden_grad * slope[...]).astype(BF)


def weight_grad_kernel(count, pairs, *refs):
    lefts_rights, outs = refs[: 2 * pairs], refs[2 * pairs :]
    for step in range(count):

        @pl.when(pl.program_id(0) == step)
        def _():
            begin = 0
            for pair in range(pairs):
                left, right = lefts_rights[2 * pair], lefts_rights[2 * pair + 1]
                made = lax.dot_general(left[...], right[...], FIRST, preferred_element_type=F32)
                width = made.shape[1]
                outs[step][:, begin : begin + width] = made.astype(outs[step].dtype)
                begin += width


def back_kernel(pack_count, pack_table, up_table, pieces, *refs):
    act, params, project, expand, *shards = refs[: -8 - len(pieces)]
    project_shards, up_shards = shards[:pack_count], shards[pack_count:]
    outs = refs[-8 - len(pieces) : -8]
    gains, project_bias, up_bias, project_whole, up_whole, project_sems, up_sems, tile = refs[-8:]

    @pl.when(pl.program_id(0) == 0)
    def _():
        columns = pl.ds(0, project_whole.shape[1])
        load_shards(project_shards, pack_table, project_whole, project_sems, 0, columns)
        load_shards(up_shards, up_table, up_whole, up_sems, 0)
        gains[...] = jnp.zeros_like(gains)
        project_bias[...] = jnp.zeros_like(project_bias)
        up_bias[...] = jnp.zeros_like(up_bias)

    normed, inverse_scale = normalize(act[...])
    first = lax.dot_general(project[...], project_whole[...], LAST, preferred_element_type=F32)
    second = lax.dot_general(expand[...], up_whole[...], LAST, preferred_element_type=F32)
    gains[0:1, :] += jnp.sum(first * normed, axis=0, keepdims=True)
    gains[1:2, :] += jnp.sum(first, axis=0, keepdims=True)
    gains[2:3, :] += jnp.sum(second * normed, axis=0, keepdims=True)
    gains[3:4, :] += jnp.sum(second, axis=0, keepdims=True)
    project_bias[...] += jnp.sum(project[...].astype(F32), axis=0, keepdims=True)
    up_bias[...] += jnp.sum(expand[...].astype(F32), axis=0, keepdims=True)
    normed_grad = first * params[0:1, :] + second * params[2:3, :]
    mean_grad = jnp.mean(normed_grad, axis=1, keepdims=True)
    mean_product = jnp.mean(normed_grad * normed, axis=1, keepdims=True)
    result = (inverse_scale * (normed_grad - mean_grad - normed * mean_product)).astype(BF)
    if pieces == [None]:
        outs[0][...] = result
        return
    tile[...] = result
    place, width = lax.axis_index("row"), tile.shape[1] // 8
    for out, masks in zip(outs, pieces):
        for at, mask in enumerate(masks):
            source = pl.ds(pl.multiple_of((place ^ mask) * width, width), width)
            out[:, at * width : (at + 1) * width] = tile[:, source]


def tile_spec(width, tile=TILE):
    return pl.BlockSpec((tile, width), lambda i: (i, 0))


def fixed_spec(shape):
    return pl.BlockSpec(shape, lambda i: (0, 0))


ANY = pl.BlockSpec(memory_space=pl.ANY)


def shape_of(shape, kind):
    return jax.ShapeDtypeStruct(shape, kind)


def cost(flops, moved=0):
    return pl.CostEstimate(flops=int(flops), bytes_accessed=int(moved), transcendentals=0)


def call(kernel, name, tokens, ins, outs, wholes, args, moved=0, tile=TILE):
    scratch = [pltpu.VMEM(shape, BF) for shape, _ in wholes] + [
        pltpu.SemaphoreType.DMA((count,)) for _, count in wholes
    ]
    return pl.pallas_call(
        kernel,
        name=name,
        grid=(tokens // tile,),
        in_specs=ins,
        out_specs=[spec for spec, _ in outs],
        out_shape=[shape for _, shape in outs],
        scratch_shapes=scratch,
        compiler_params=pltpu.CompilerParams(
            dimension_semantics=("arbitrary",), vmem_limit_bytes=VMEM_LIMIT
        ),
        cost_estimate=cost(sum(2 * tokens * shape[0] * shape[1] for shape, _ in wholes), moved),
    )(*args)


def weight_grad(count, place, pairs, chunked_right=False):
    specs, arrays, width = [], [], 0
    for left, right in pairs:
        chunked, fixed = (right, left) if chunked_right else (left, right)
        extent = chunked.shape[1] // count
        chunk_spec = pl.BlockSpec(
            (chunked.shape[0], extent), lambda i, spot: (0, lax.rem(spot[0] + i, count))
        )
        fixed_spec_ = pl.BlockSpec(fixed.shape, lambda i, spot: (0, 0))
        specs += [fixed_spec_, chunk_spec] if chunked_right else [chunk_spec, fixed_spec_]
        arrays += [left, right]
        rows, columns = (fixed.shape[1], extent) if chunked_right else (extent, fixed.shape[1])
        width += columns
    shape = (rows, width)
    return pl.pallas_call(
        functools.partial(drop_first, functools.partial(weight_grad_kernel, count, len(pairs))),
        name="weight_grad",
        grid_spec=pltpu.PrefetchScalarGridSpec(
            num_scalar_prefetch=1,
            grid=(count,),
            in_specs=specs,
            out_specs=[pl.BlockSpec(shape, lambda i, spot: (0, 0))] * count,
        ),
        out_shape=[shape_of(shape, F32 if r == 0 else BF) for r in range(count)],
        compiler_params=pltpu.CompilerParams(
            dimension_semantics=("arbitrary",), vmem_limit_bytes=VMEM_LIMIT
        ),
        cost_estimate=cost(2 * arrays[0].shape[0] * rows * width * count),
    )(place[None], *arrays)


def drop_first(kernel, spot, *refs):
    kernel(*refs)


def angle_tables(row_total):
    positions = (jnp.arange(row_total, dtype=jnp.int32) % LENGTH).astype(F32)
    frequency = ROPE_BASE ** (-jnp.arange(0, ROTARY, 2, dtype=jnp.int32).astype(F32) / ROTARY)
    turning = positions[:, None] * frequency[None, :]
    cosine, sine = jnp.cos(turning), jnp.sin(turning)
    rest = HEAD_DIM - ROTARY
    zeros = jnp.zeros_like(sine)
    return (
        jnp.concatenate([cosine, cosine, jnp.ones((row_total, rest), F32)], axis=1),
        jnp.concatenate([-sine, zeros, jnp.zeros((row_total, rest), F32)], axis=1),
        jnp.concatenate([zeros, sine, jnp.zeros((row_total, rest), F32)], axis=1),
    )


def on_device(
    rows,
    cols,
    activations,
    document_ids,
    attention_gain,
    attention_shift,
    feedforward_gain,
    feedforward_shift,
    query_key_value,
    query_key_value_bias,
    output_weight,
    output_bias,
    up_weight,
    up_bias,
    down_weight,
    down_bias,
    out_grad,
):
    row_place, col_place = lax.axis_index("row"), lax.axis_index("col")
    tokens, features = activations.shape
    heads = query_key_value.shape[1]
    project_width, out_width = heads * 3 * HEAD_DIM, heads * HEAD_DIM
    hidden_width = up_weight.shape[1]

    full_input = lax.all_gather(activations, "row", axis=1, tiled=True)
    full_grad = lax.all_gather(out_grad, "row", axis=1, tiled=True)

    pack = jnp.concatenate(
        [query_key_value.astype(BF).reshape(-1, project_width), output_weight.astype(BF).T], axis=1
    )
    pack_gather = RingGather(pack, cols)
    down_shard = down_weight.astype(BF).T
    up_shard = up_weight.astype(BF)
    up_gather = RingGather(up_shard, cols)
    both = LineBoth(down_shard, col_place) if cols == 4 else None
    down_gather = both or RingGather(down_shard, cols)

    def slot(transfers, gate, *works):
        moved = []
        for transfer in transfers:
            moved += transfer.step(gate)
        made = [work(gate) for work in works]
        return moved + [array for arrays in made for array in arrays], made

    def more(transfers, gate):
        for _ in range(cols - 4):
            gate, _ = slot(transfers, gate)
        return gate

    def tables_work(gate):
        cosine, left, right = angle_tables(tokens)
        starts = jnp.sum(
            (document_ids[:, None] < document_ids[None, :]).astype(jnp.int32), axis=0
        )
        sums = jnp.sum(out_grad.astype(F32), axis=0)
        return cosine, left, right, starts, sums, down_shard, up_shard

    def params_work(gate):
        stacked = jnp.stack(
            [attention_gain, attention_shift, feedforward_gain, feedforward_shift]
        )
        return [lax.all_gather(after(stacked, gate), "row", axis=1, tiled=True)]

    def norm_work(gate):
        return call(
            norm_kernel,
            "norm",
            tokens,
            [tile_spec(D), fixed_spec((4, D))],
            [
                (tile_spec(D), shape_of((tokens, D), BF)),
                (tile_spec(D), shape_of((tokens, D), BF)),
            ],
            [],
            [full_input, after(norm_params, gate)],
            6 * tokens * D,
        )

    gate, ((cosine, left, right, starts, shift_out_grad, *_),) = slot([pack_gather], [], tables_work)
    low_blocks = starts[::QUERY_BLOCK] // KEY_BLOCK
    high_blocks = (starts[QUERY_BLOCK - 1 :: QUERY_BLOCK] + KEY_BLOCK - 1) // KEY_BLOCK
    gate, ((norm_params,),) = slot([pack_gather], gate, params_work)
    gate = more([pack_gather], gate)
    gate, ((first_norm, second_norm),) = slot([pack_gather], gate, norm_work)
    pack_shards, pack_table = pack_gather.shards()

    def project_work(gate):
        return call(
            functools.partial(project_kernel, pack_table, heads),
            "project",
            tokens,
            [tile_spec(D), fixed_spec((1, project_width))]
            + [tile_spec(HEAD_DIM)] * 3
            + [ANY] * len(pack_shards),
            [(tile_spec(project_width), shape_of((tokens, project_width), BF))],
            [((D, project_width), cols)],
            [
                after(first_norm, gate),
                query_key_value_bias.reshape(1, -1),
                cosine,
                left,
                right,
                *pack_shards,
            ],
        )

    def attended_grad_work(gate):
        return call(
            functools.partial(attended_grad_kernel, pack_table),
            "attended_grad",
            tokens,
            [tile_spec(D, 4 * TILE)] + [ANY] * len(pack_shards),
            [(tile_spec(out_width, 4 * TILE), shape_of((tokens, out_width), BF))],
            [((D, out_width), cols)],
            [after(full_grad, gate), *pack_shards],
            tile=4 * TILE,
        )

    def whole_spec(*shape):
        return pl.BlockSpec(shape, lambda i: (0, 0))

    def attention_work(projected, head, before):
        def column_spec(width):
            return pl.BlockSpec((tokens, width), lambda i: (0, head))

        return pl.pallas_call(
            attention_kernel,
            name="attention",
            grid=(1,),
            in_specs=[pl.BlockSpec(memory_space=pltpu.SMEM)] * 2
            + [whole_spec(1, tokens), column_spec(3 * HEAD_DIM)]
            + [ANY] * len(before),
            out_specs=[column_spec(HEAD_DIM), whole_spec(HEAD_DIM, tokens), whole_spec(1, tokens)],
            out_shape=[
                shape_of((tokens, out_width), BF),
                shape_of((HEAD_DIM, tokens), F32),
                shape_of((1, tokens), F32),
            ],
            input_output_aliases={4: 0} if before else {},
            scratch_shapes=[pltpu.VMEM((HEAD_DIM, tokens), BF)],
            compiler_params=pltpu.CompilerParams(vmem_limit_bytes=VMEM_LIMIT),
            cost_estimate=cost(8 * tokens * tokens * HEAD_DIM),
        )(low_blocks, high_blocks, starts[None], projected, *before)

    def attention_back_work(gate):
        return pl.pallas_call(
            functools.partial(attention_back_kernel, heads),
            name="attention_back",
            grid=(1,),
            in_specs=[pl.BlockSpec(memory_space=pltpu.SMEM)] * 2
            + [whole_spec(1, tokens)]
            + [whole_spec(tokens, HEAD_DIM)] * 3
            + [whole_spec(tokens, project_width), whole_spec(tokens, out_width)]
            + [whole_spec(HEAD_DIM, tokens)] * heads
            + [whole_spec(1, tokens)] * heads,
            out_specs=[whole_spec(tokens, project_width)],
            out_shape=[shape_of((tokens, project_width), BF)],
            scratch_shapes=[pltpu.VMEM((heads, HEAD_DIM, tokens), BF)]
            + [pltpu.VMEM((heads, tokens, HEAD_DIM), F32)] * 2,
            compiler_params=pltpu.CompilerParams(vmem_limit_bytes=VMEM_LIMIT),
            cost_estimate=cost(16 * tokens * tokens * out_width),
        )(
            low_blocks,
            high_blocks,
            starts[None],
            cosine,
            left,
            right,
            projected,
            after(attended_grad, gate),
            *[made[1] for made in by_head],
            *[made[2] for made in by_head],
        )

    by_head = []

    def first_head_work(gate):
        (projected,) = project_work(gate)
        by_head.append(attention_work(projected, 0, []))
        return projected, by_head[0][2]

    gate, ((projected, _),) = slot([up_gather], gate, first_head_work)

    def other_heads_work(gate):
        values = after(projected, gate)
        for head in range(1, heads):
            by_head.append(attention_work(values, head, [by_head[-1][0]]))
        return attended_grad_work(gate + [by_head[-1][2]])

    gate, ((attended_grad,),) = slot([up_gather], gate, other_heads_work)
    attended = by_head[-1][0]
    gate = more([up_gather], gate)
    gate, ((project_grad,),) = slot([up_gather], gate, attention_back_work)
    up_shards, up_table = up_gather.shards()

    def pack_weight_work(gate):
        return weight_grad(
            cols, col_place, [(first_norm, after(project_grad, gate)), (full_grad, attended)]
        )

    def up_work(gate):
        return call(
            functools.partial(up_kernel, up_table),
            "up",
            tokens,
            [tile_spec(D, 2 * TILE), fixed_spec((1, hidden_width))] + [ANY] * len(up_shards),
            [
                (tile_spec(hidden_width, 2 * TILE), shape_of((tokens, hidden_width), BF)),
                (tile_spec(hidden_width, 2 * TILE), shape_of((tokens, hidden_width), F32)),
            ],
            [((D, hidden_width), cols)],
            [after(second_norm, gate), up_bias[None], *up_shards],
            tile=2 * TILE,
        )

    def down_weight_work(gate):
        return weight_grad(cols, col_place, [(after(hidden, gate), full_grad)], True)

    gate, (pack_chunks,) = slot([down_gather], gate, pack_weight_work)
    gate = more([down_gather], gate)
    if both is not None:
        both.chunks = pack_chunks
    gate, ((hidden, slope),) = slot([down_gather], gate, up_work)
    gate, (down_chunks,) = slot([down_gather], gate, down_weight_work)
    down_shards, down_table = down_gather.shards()
    pack_scatter = both or RingScatter(pack_chunks, cols)
    down_scatter = RingScatter(down_chunks, cols)
    if both is None:
        for _ in range(cols - 2):
            gate, _ = slot([pack_scatter], gate)

    def mixed_work(gate):
        return call(
            functools.partial(mixed_kernel, len(pack_shards), pack_table, down_table),
            "mixed",
            tokens,
            [tile_spec(out_width, 2 * TILE), tile_spec(hidden_width, 2 * TILE)] + [ANY] * (len(pack_shards) + len(down_shards)),
            [(tile_spec(D, 2 * TILE), shape_of((tokens, D), BF))],
            [((D, out_width), cols), ((D, hidden_width), cols)],
            [after(attended, gate), hidden, *pack_shards, *down_shards],
            tile=2 * TILE,
        )

    def hidden_grad_work(gate):
        return call(
            functools.partial(hidden_grad_kernel, down_table),
            "hidden_grad",
            tokens,
            [tile_spec(D, 2 * TILE), tile_spec(hidden_width, 2 * TILE)] + [ANY] * len(down_shards),
            [(tile_spec(hidden_width, 2 * TILE), shape_of((tokens, hidden_width), BF))],
            [((D, hidden_width), cols)],
            [after(full_grad, gate), slope, *down_shards],
            tile=2 * TILE,
        )

    pieces = [RowScatter.KEPT, RowScatter.SENT] if rows == 8 else [None]

    def back_work(gate):
        widths = project_width, hidden_width
        share = D // len(pieces)
        return pl.pallas_call(
            functools.partial(back_kernel, len(pack_shards), pack_table, up_table, pieces),
            name="back",
            grid=(tokens // TILE,),
            in_specs=[tile_spec(D), fixed_spec((4, D)), *map(tile_spec, widths)]
            + [ANY] * (len(pack_shards) + len(up_shards)),
            out_specs=[tile_spec(share)] * len(pieces)
            + [fixed_spec((4, D)), *[fixed_spec((1, width)) for width in widths]],
            out_shape=[shape_of((tokens, share), BF)] * len(pieces)
            + [shape_of((4, D), F32), *[shape_of((1, width), F32) for width in widths]],
            scratch_shapes=[pltpu.VMEM((D, width), BF) for width in widths]
            + [pltpu.SemaphoreType.DMA((cols,))] * 2
            + [pltpu.VMEM((TILE, D), BF)],
            compiler_params=pltpu.CompilerParams(
                dimension_semantics=("arbitrary",), vmem_limit_bytes=VMEM_LIMIT
            ),
            cost_estimate=cost(2 * tokens * D * sum(widths)),
        )(
            full_input,
            norm_params,
            project_grad,
            after(expand_grad, gate),
            *pack_shards,
            *up_shards,
        )

    def up_weight_work(gate):
        return weight_grad(cols, col_place, [(second_norm, after(expand_grad, gate))])

    def down_result_work(gate):
        return [down_scatter.result(gate)]

    def layer_out_work(gate):
        return [
            activations.astype(F32) + after(mixed_sum, gate).astype(F32) + output_bias + down_bias
        ]

    gate, ((mixed_part,),) = slot([pack_scatter], gate, mixed_work)
    mixed_sum = lax.psum_scatter(after(mixed_part, gate), "row", scatter_dimension=1, tiled=True)
    gate, ((expand_grad,),) = slot([down_scatter], gate, hidden_grad_work)
    gate = more([down_scatter], gate)
    gate, (up_chunks,) = slot([down_scatter], gate, up_weight_work)
    up_scatter = RingScatter(up_chunks, cols)
    gate, ((*back_parts, gains, project_bias_grad, up_bias_grad),) = slot(
        [down_scatter, up_scatter], gate, back_work
    )

    def split_work(gate):
        parts = pack_scatter.result(gate)
        shape = query_key_value.shape
        return parts[:, :project_width].reshape(shape), parts[:, project_width:].T

    def gains_work(gate):
        terms = after(gains, gate)
        terms = terms.reshape(4, rows, features).transpose(1, 0, 2).reshape(rows, -1)
        return [pair_scatter(terms, "row", rows, row_place)]

    row_scatter = RowScatter(*back_parts) if rows == 8 else None
    row_steps = [row_scatter] if rows == 8 else []

    for step in row_steps + [up_scatter]:
        step.step(gate)
    (gain_terms,) = gains_work(gate + [up_scatter.sent])
    (down_weight_grad,) = down_result_work(gate)
    project_weight_grad, output_weight_grad = split_work(gate)
    for step in row_steps:
        step.step([])
    small = [gain_terms, project_bias_grad[0], up_bias_grad[0], shift_out_grad]
    masks = [1 << bit for bit in range(cols.bit_length() - 1)]
    gate = row_scatter.parts if row_scatter is not None else []
    small = pair_sum(jnp.concatenate(small), "col", cols, masks[:-1], gate)
    gate = gate + [down_weight_grad, project_weight_grad, output_weight_grad, small]
    for _ in range(cols - 3):
        up_scatter.step(gate)
    (layer_out,) = layer_out_work([up_scatter.sent])
    arrived = pair_exchange(small, "col", cols, masks[-1], [up_scatter.sent])
    for step in row_steps:
        step.step([up_scatter.sent])
    up_weight_grad = up_scatter.result([layer_out])
    if row_scatter is not None:
        back_sum = row_scatter.result()
    else:
        back_sum = lax.psum_scatter(back_parts[0], "row", scatter_dimension=1, tiled=True)
    activations_grad = after(out_grad, [up_weight_grad]).astype(F32) + back_sum.astype(F32)
    small = after(small, [activations_grad]) + arrived
    sizes = [features] * 4 + [project_width, hidden_width, features]
    pieces, begin = [], 0
    for size in sizes:
        pieces.append(small[begin : begin + size])
        begin += size
    return (
        layer_out,
        activations_grad,
        pieces[0],
        pieces[1],
        pieces[2],
        pieces[3],
        project_weight_grad,
        pieces[4].reshape(query_key_value_bias.shape),
        output_weight_grad,
        pieces[6],
        up_weight_grad,
        pieces[5],
        down_weight_grad,
        pieces[6],
    )


def solution(mesh):
    placed = (
        P("col", "row"),
        P("col"),
        P("row"),
        P("row"),
        P("row"),
        P("row"),
        P("col", "row", None),
        P("row", None),
        P("row", "col"),
        P("row"),
        P("col", "row"),
        P("row"),
        P("row", "col"),
        P("row"),
        P("col", "row"),
    )

    def body(*args):
        return on_device(mesh.shape["row"], mesh.shape["col"], *args)

    return jax.shard_map(
        body,
        mesh=mesh,
        in_specs=placed,
        out_specs=(
            P("col", "row"),
            P("col", "row"),
            P("row"),
            P("row"),
            P("row"),
            P("row"),
            P("col", "row", None),
            P("row", None),
            P("row", "col"),
            P("row"),
            P("col", "row"),
            P("row"),
            P("row", "col"),
            P("row"),
        ),
        check_vma=False,
    )
```

profile of v0, /device:TPU:0, one launch (start us, length us, event | category | flops | bytes accessed | tf_op | source)
XLA Modules:
  0.0 442.1 jit_solution(10080189542952365719)
XLA Ops:
  15.7 5.4 %multiply_sine_fusion = (f32[2048,16]{1,0:T(8,128)S(1)}, f32[2048,16]{1,0:T(8,128)}, f32[2048,16]{1,0:T(8,128)S(1)}) fusion(f32[2048]{0:T(1024)S(1)} %fusion.5, f32[16]{0:T(128)S(1)} %multiply_power_fusion), kind=kLoop, calls=%fused_computation.22 | loop fusion | flops 65536 | bytes 401472 | tf_op jit(solution)/shard_map/sin | solution.py:546
  30.3 9.2 %collective-permute-done.refs_6_.refs_2_.refs_3_.refs_5_ = bf16[512,1024]{1,0:T(8,128)(2,1)} collective-permute-done((bf16[512,1024]{1,0:T(8,128)(2,1)}, bf16[512,1024]{1,0:T(8,128)(2,1)}, u32[]{:S(2)}, u32[]{:S(2)}) %collective-permute-start) | collective-permute-done | bytes 1048608 | tf_op jit(solution)/shard_map/ppermute | solution.py:41
  39.5 10.2 %all_gather.10.params.refs_1_ = f32[4,2048]{1,0:T(4,128)} all-gather(f32[4,256]{1,0:T(4,128)S(1)} %pad_maximum_fusion.2), channel_id=1, replica_groups=mesh['row'=8,'col'=4] {'row'}, dimensions={1}, use_global_device_ids=true | all-gather | bytes 36864 | tf_op jit(solution)/shard_map/all_gather | solution.py:618
  49.7 16.1 %collective-permute-done.1.refs_7_.refs_3_.refs_4_.refs_6_ = bf16[512,1024]{1,0:T(8,128)(2,1)S(1)} collective-permute-done((bf16[512,1024]{1,0:T(8,128)(2,1)}, bf16[512,1024]{1,0:T(8,128)(2,1)S(1)}, u32[]{:S(2)}, u32[]{:S(2)}) %collective-permute-start.1) | collective-permute-done | bytes 1048608 | tf_op jit(solution)/shard_map/ppermute | solution.py:41
  68.7 13.9 %norm.1 = (bf16[2048,2048]{1,0:T(8,128)(2,1)}, bf16[2048,2048]{1,0:T(8,128)(2,1)}) custom-call(bf16[2048,2048]{1,0:T(8,128)(2,1)} %all-gather.3.cloned.1.call-done.act.refs_0_, f32[4,2048]{1,0:T(4,128)} %all_gather.10.params.refs_1_), custom_call_target="tpu_custom_call" | custom-call | bytes 25165824 | tf_op jit(solution)/shard_map/norm/pallas_call | solution.py:492
  82.6 8.6 %collective-permute-done.2.refs_8_.refs_4_.refs_5_.refs_7_ = bf16[512,1024]{1,0:T(8,128)(2,1)} collective-permute-done((bf16[512,1024]{1,0:T(8,128)(2,1)S(1)}, bf16[512,1024]{1,0:T(8,128)(2,1)}, u32[]{:S(2)}, u32[]{:S(2)}) %collective-permute-start.2) | collective-permute-done | bytes 1048608 | tf_op jit(solution)/shard_map/ppermute | solution.py:41
  92.3 14.8 %project.1 = bf16[2048,768]{1,0:T(8,128)(2,1)} custom-call(bf16[2048,2048]{1,0:T(8,128)(2,1)} %get-tuple-element.91.refs_0_, f32[1,768]{1,0:T(1,128)} %bitcast.47, f32[2048,128]{1,0:T(8,128)} %maximum_maximum_fusion.refs_2_.cosine, f32[2048,128]{1,0:T(8,128)} %get-tuple-element.201.refs_3_.left, f32[2048,128]{1,0:T(8,128)} %get-tuple-element.200.refs_4_.right, ...), custom_call_target="tpu_custom_call" | custom-call | flops 6442450944 | tf_op jit(solution)/shard_map/project/pallas_call | solution.py:492
  107.1 9.0 %attention.2 = (bf16[2048,256]{1,0:T(8,128)(2,1)}, f32[128,2048]{1,0:T(8,128)}, f32[1,2048]{1,0:T(1,128)}) custom-call(s32[4]{0:T(128)} %get-tuple-element.217.low, s32[4]{0:T(128)} %get-tuple-element.216.high, s32[1,2048]{1,0:T(1,128)} %bitcast.53, bf16[2048,768]{1,0:T(8,128)(2,1)} %project.1), custom_call_target="tpu_custom_call" | custom-call | flops 4294967296 | tf_op jit(solution)/shard_map/attention/pallas_call | solution.py:682
  116.3 9.1 %attention.3 = (bf16[2048,256]{1,0:T(8,128)(2,1)}, f32[128,2048]{1,0:T(8,128)}, f32[1,2048]{1,0:T(1,128)}) custom-call(s32[4]{0:T(128)} %get-tuple-element.217.low, s32[4]{0:T(128)} %get-tuple-element.216.high, s32[1,2048]{1,0:T(1,128)} %bitcast.54, bf16[2048,768]{1,0:T(8,128)(2,1)} %project.1, ...), custom_call_target="tpu_custom_call", output_to_operand_aliasing={{0}: (4, {})} | custom-call | flops 4294967296 | tf_op jit(solution)/shard_map/attention/pallas_call | solution.py:682
  126.5 7.2 %attended_grad.1.grad = bf16[2048,256]{1,0:T(8,128)(2,1)} custom-call(bf16[2048,2048]{1,0:T(8,128)(2,1)} %all-gather.5.cloned.1.call-done.refs_0_.refs_2_.refs_1_, bf16[512,1024]{1,0:T(8,128)(2,1)} %pad_maximum_fusion.refs_5_.refs_1_.refs_2_.refs_4_, bf16[512,1024]{1,0:T(8,128)(2,1)} %collective-permute-done.refs_6_.refs_2_.refs_3_.refs_5_, ...), custom_call_target="tpu_custom_call" | custom-call | flops 2147483648 | tf_op jit(solution)/shard_map/attended_grad/pallas_call | solution.py:492
  133.8 8.4 %collective-permute-done.4.refs_4_.refs_10_ = bf16[512,1024]{1,0:T(8,128)(2,1)S(1)} collective-permute-done((bf16[512,1024]{1,0:T(8,128)(2,1)S(1)}, bf16[512,1024]{1,0:T(8,128)(2,1)S(1)}, u32[]{:S(2)}, u32[]{:S(2)}) %collective-permute-start.4) | collective-permute-done | bytes 1048608 | tf_op jit(solution)/shard_map/ppermute | solution.py:41
  142.2 23.9 %attention_back.1.refs_1_.refs_2_ = bf16[2048,768]{1,0:T(8,128)(2,1)} custom-call(s32[4]{0:T(128)} %get-tuple-element.217.low, s32[4]{0:T(128)} %get-tuple-element.216.high, s32[1,2048]{1,0:T(1,128)} %bitcast.55, f32[2048,128]{1,0:T(8,128)} %maximum_maximum_fusion.refs_2_.cosine, f32[2048,128]{1,0:T(8,128)} %get-tuple-element.201.refs_3_.left, ...), custom_call_target="tpu_custom_call" | custom-call | flops 17179869184 | tf_op jit(solution)/shard_map/attention_back/pallas_call | solution.py:702
  167.0 3.8 collective-permute-start.6
  172.5 15.4 %weight_grad.3 = (f32[512,1024]{1,0:T(8,128)}, bf16[512,1024]{1,0:T(8,128)(2,1)}, bf16[512,1024]{1,0:T(8,128)(2,1)}, bf16[512,1024]{1,0:T(8,128)(2,1)}) custom-call(s32[1]{0:T(128)} %bitcast.7.spot, bf16[2048,2048]{1,0:T(8,128)(2,1)} %get-tuple-element.91.refs_0_, bf16[2048,768]{1,0:T(8,128)(2,1)} %attention_back.1.refs_1_.refs_2_, ...), custom_call_target="tpu_custom_call" | custom-call | flops 8589934592 | tf_op jit(solution)/shard_map/weight_grad/pallas_call | solution.py:521
  193.0 7.9 %collective-permute-start.8 = (bf16[512,1024]{1,0:T(8,128)(2,1)}, bf16[512,1024]{1,0:T(8,128)(2,1)}, u32[]{:S(2)}, u32[]{:S(2)}) collective-permute-start(bf16[512,1024]{1,0:T(8,128)(2,1)} %broadcast_select_fusion.1), channel_id=1, source_target_pairs={{0,1},{1,2},{2,3},{4,5},{5,6},{6,7},{8,9},{9,10},{10,11},{12,13},{... | collective-permute-start | bytes 3145736 | tf_op jit(solution)/shard_map/ppermute | solution.py:86
  202.4 17.8 %up.1 = (bf16[2048,1024]{1,0:T(8,128)(2,1)}, f32[2048,1024]{1,0:T(8,128)}) custom-call(bf16[2048,2048]{1,0:T(8,128)(2,1)} %get-tuple-element.112.refs_0_, f32[1,1024]{1,0:T(1,128)} %bitcast.52, bf16[512,1024]{1,0:T(8,128)(2,1)} %convert_element_type.184.refs_2_.refs_8_, bf16[512,1024]{1,0:T(8,128)(2,1)} %copy-done.31, bf16[512,1024]{1,0:T(8,128)(2,1)} %copy-done.32, ...), custom_call_target="tpu_custom_call" | custom-call | flops 8589934592 | tf_op jit(solution)/shard_map/up/pallas_call | solution.py:492
  220.2 3.1 collective-permute-done.9.refs_11_.refs_7_
  223.3 3.5 fusion.2
  228.2 4.9 %collective-permute-start.10 = (bf16[512,1024]{1,0:T(8,128)(2,1)S(1)}, bf16[512,1024]{1,0:T(8,128)(2,1)S(1)}, u32[]{:S(2)}, u32[]{:S(2)}) collective-permute-start(bf16[512,1024]{1,0:T(8,128)(2,1)S(1)} %get-tuple-element.115), channel_id=1, source_target_pairs={{0,1},{1,2},{2,3},{4,5},{5,6},{6,7},{8,9},{9,10},{10,11},{12,13},{... | collective-permute-start | bytes 3145736 | tf_op jit(solution)/shard_map/ppermute | solution.py:86
  233.1 14.8 %weight_grad.4 = (f32[1024,512]{1,0:T(8,128)}, bf16[1024,512]{1,0:T(8,128)(2,1)}, bf16[1024,512]{1,0:T(8,128)(2,1)}, bf16[1024,512]{1,0:T(8,128)(2,1)}) custom-call(s32[1]{0:T(128)} %bitcast.7.spot, bf16[2048,1024]{1,0:T(8,128)(2,1)} %get-tuple-element.117.refs_0_.refs_1_, bf16[2048,2048]{1,0:T(8,128)(2,1)} %all-gather.5.cloned.1.call-done.refs_0_.refs_2_.refs_1_), custom_call_target="tpu_custom_call" | custom-call | flops 8589934592 | tf_op jit(solution)/shard_map/weight_grad/pallas_call | solution.py:521
  252.4 4.9 %collective-permute-start.12 = (bf16[512,1024]{1,0:T(8,128)(2,1)}, bf16[512,1024]{1,0:T(8,128)(2,1)S(1)}, u32[]{:S(2)}, u32[]{:S(2)}) collective-permute-start(bf16[512,1024]{1,0:T(8,128)(2,1)} %add_convert_fusion.8), channel_id=1, source_target_pairs={{0,1},{1,2},{2,3},{4,5},{5,6},{6,7},{8,9},{9,10},{10,11},{12,13},{... | collective-permute-start | bytes 3145736 | tf_op jit(solution)/shard_map/ppermute | solution.py:86
  257.3 18.0 %mixed.1 = bf16[2048,2048]{1,0:T(8,128)(2,1)} custom-call(bf16[2048,256]{1,0:T(8,128)(2,1)} %get-tuple-element.122.refs_3_.refs_0_, bf16[2048,1024]{1,0:T(8,128)(2,1)} %get-tuple-element.117.refs_0_.refs_1_, bf16[512,1024]{1,0:T(8,128)(2,1)} %pad_maximum_fusion.refs_5_.refs_1_.refs_2_.refs_4_, ...), custom_call_target="tpu_custom_call" | custom-call | flops 10737418240 | tf_op jit(solution)/shard_map/mixed/pallas_call | solution.py:492
  279.0 17.4 %hidden_grad.1.refs_1_.refs_3_ = bf16[2048,1024]{1,0:T(8,128)(2,1)} custom-call(bf16[2048,2048]{1,0:T(8,128)(2,1)} %all-gather.5.cloned.1.call-done.refs_0_.refs_2_.refs_1_, f32[2048,1024]{1,0:T(8,128)} %get-tuple-element.114.refs_1_, bf16[512,1024]{1,0:T(8,128)(2,1)} %bitcast.34, bf16[512,1024]{1,0:T(8,128)(2,1)} %collective-permute-done.6.refs_7_.refs_3_, ...), custom_call_target="tpu_custom_call" | custom-call | flops 8589934592 | tf_op jit(solution)/shard_map/hidden_grad/pallas_call | solution.py:492
  296.4 3.7 collective-permute-done.14
  302.3 14.8 %weight_grad.5 = (f32[512,1024]{1,0:T(8,128)}, bf16[512,1024]{1,0:T(8,128)(2,1)}, bf16[512,1024]{1,0:T(8,128)(2,1)}, bf16[512,1024]{1,0:T(8,128)(2,1)}) custom-call(s32[1]{0:T(128)} %bitcast.7.spot, bf16[2048,2048]{1,0:T(8,128)(2,1)} %get-tuple-element.112.refs_0_, bf16[2048,1024]{1,0:T(8,128)(2,1)} %hidden_grad.1.refs_1_.refs_3_), custom_call_target="tpu_custom_call" | custom-call | flops 8589934592 | tf_op jit(solution)/shard_map/weight_grad/pallas_call | solution.py:521
  317.1 6.2 %collective-permute-done.15 = bf16[1024,512]{1,0:T(8,128)(2,1)S(1)} collective-permute-done((bf16[1024,512]{1,0:T(8,128)(2,1)S(1)}, bf16[1024,512]{1,0:T(8,128)(2,1)S(1)}, u32[]{:S(2)}, u32[]{:S(2)}) %collective-permute-start.15) | collective-permute-done | bytes 1048608 | tf_op jit(solution)/shard_map/ppermute | solution.py:62
  327.3 35.4 %back.1 = (bf16[2048,1024]{1,0:T(8,128)(2,1)}, bf16[2048,1024]{1,0:T(8,128)(2,1)}, f32[4,2048]{1,0:T(4,128)}, f32[1,768]{1,0:T(1,128)}, f32[1,1024]{1,0:T(1,128)}) custom-call(bf16[2048,2048]{1,0:T(8,128)(2,1)} %all-gather.3.cloned.1.call-done.act.refs_0_, f32[4,2048]{1,0:T(4,128)} %all_gather.10.params.refs_1_, ...), custom_call_target="tpu_custom_call" | custom-call | flops 15032385536 | tf_op jit(solution)/shard_map/back/pallas_call | solution.py:817
  384.6 10.6 %collective-permute-done.22 = f32[3072]{0:T(1024)S(1)} collective-permute-done((f32[3072]{0:T(1024)S(1)}, f32[3072]{0:T(1024)S(1)}, u32[]{:S(2)}, u32[]{:S(2)}) %collective-permute-start.22) | collective-permute-done | bytes 12320 | tf_op jit(solution)/shard_map/ppermute | solution.py:146
  398.4 4.2 add_convert_fusion.1
  407.9 3.0 add_add_fusion.1
  411.0 14.8 %collective-permute-done.24 = bf16[512,1024]{1,0:T(8,128)(2,1)} collective-permute-done((bf16[512,1024]{1,0:T(8,128)(2,1)}, bf16[512,1024]{1,0:T(8,128)(2,1)}, u32[]{:S(2)}, u32[]{:S(2)}) %collective-permute-start.24) | collective-permute-done | bytes 1048608 | tf_op jit(solution)/shard_map/ppermute | solution.py:62
  428.6 4.1 add_add_fusion
  (185 shorter events, 83.1 us)
Async XLA Ops:
  7.2 61.5 %all-gather.3.cloned.1.call-start = ((), (), s32[]{:S(2)}) async-start(), calls=%async_computation.1 | async-start | bytes 9437184 | tf_op jit(solution)/shard_map/all_gather | solution.py:581
  7.9 118.6 %all-gather.5.cloned.1.call-start = ((), (), s32[]{:S(2)}) async-start(), calls=%async_computation.2 | async-start | bytes 9437184 | tf_op jit(solution)/shard_map/all_gather | solution.py:582
  8.7 399.2 %reduce-scatter.2.cloned.1.call-start = ((), (), s32[]{:S(2)}) async-start(), calls=%async_computation.3 | async-start | bytes 9437184 | tf_op jit(solution)/shard_map/reduce_scatter | solution.py:855
  11.0 28.5 %collective-permute-start = (bf16[512,1024]{1,0:T(8,128)(2,1)}, bf16[512,1024]{1,0:T(8,128)(2,1)}, u32[]{:S(2)}, u32[]{:S(2)}) collective-permute-start(bf16[512,1024]{1,0:T(8,128)(2,1)} %pad_maximum_fusion.refs_5_.refs_1_.refs_2_.refs_4_), channel_id=1, source_target_pairs={{0,1},{1,2},{2,3},{3,0},{4,5},{5,6},{6,7},{7,4},{8,9},{9,10},{10,1... | collective-permute-start | bytes 3145736 | tf_op jit(solution)/shard_map/ppermute | solution.py:41
  39.5 26.4 %collective-permute-start.1 = (bf16[512,1024]{1,0:T(8,128)(2,1)}, bf16[512,1024]{1,0:T(8,128)(2,1)S(1)}, u32[]{:S(2)}, u32[]{:S(2)}) collective-permute-start(bf16[512,1024]{1,0:T(8,128)(2,1)} %collective-permute-done.refs_6_.refs_2_.refs_3_.refs_5_), channel_id=1, source_target_pairs={{0,1},{1,2},{2,3},{3,0},{4,5},{5,6},{6,7},{7,4},{8,9},{9,10},{10,1... | collective-permute-start | bytes 3145736 | tf_op jit(solution)/shard_map/ppermute | solution.py:41
  65.8 25.3 %collective-permute-start.2 = (bf16[512,1024]{1,0:T(8,128)(2,1)S(1)}, bf16[512,1024]{1,0:T(8,128)(2,1)}, u32[]{:S(2)}, u32[]{:S(2)}) collective-permute-start(bf16[512,1024]{1,0:T(8,128)(2,1)S(1)} %collective-permute-done.1.refs_7_.refs_3_.refs_4_.refs_6_), channel_id=1, source_target_pairs={{0,1},{1,2},{2,3},{3,0},{4,5},{5,6},{6,7},{7,4},{8,9},{9,10},{10,1... | collective-permute-start | bytes 3145736 | tf_op jit(solution)/shard_map/ppermute | solution.py:41
  91.2 24.9 %collective-permute-start.3 = (bf16[512,1024]{1,0:T(8,128)(2,1)S(1)}, bf16[512,1024]{1,0:T(8,128)(2,1)S(1)}, u32[]{:S(2)}, u32[]{:S(2)}) collective-permute-start(bf16[512,1024]{1,0:T(8,128)(2,1)S(1)} %copy-done.9), channel_id=1, source_target_pairs={{0,1},{1,2},{2,3},{3,0},{4,5},{5,6},{6,7},{7,4},{8,9},{9,10},{10,1... | collective-permute-start | bytes 3145736 | tf_op jit(solution)/shard_map/ppermute | solution.py:41
  116.1 26.1 %collective-permute-start.4 = (bf16[512,1024]{1,0:T(8,128)(2,1)S(1)}, bf16[512,1024]{1,0:T(8,128)(2,1)S(1)}, u32[]{:S(2)}, u32[]{:S(2)}) collective-permute-start(bf16[512,1024]{1,0:T(8,128)(2,1)S(1)} %collective-permute-done.3.refs_3_.refs_9_), channel_id=1, source_target_pairs={{0,1},{1,2},{2,3},{3,0},{4,5},{5,6},{6,7},{7,4},{8,9},{9,10},{10,1... | collective-permute-start | bytes 3145736 | tf_op jit(solution)/shard_map/ppermute | solution.py:41
  142.2 23.9 %collective-permute-start.5 = (bf16[512,1024]{1,0:T(8,128)(2,1)S(1)}, bf16[512,1024]{1,0:T(8,128)(2,1)S(1)}, u32[]{:S(2)}, u32[]{:S(2)}) collective-permute-start(bf16[512,1024]{1,0:T(8,128)(2,1)S(1)} %collective-permute-done.4.refs_4_.refs_10_), channel_id=1, source_target_pairs={{0,1},{1,2},{2,3},{3,0},{4,5},{5,6},{6,7},{7,4},{8,9},{9,10},{10,1... | collective-permute-start | bytes 3145736 | tf_op jit(solution)/shard_map/ppermute | solution.py:41
  167.0 20.9 %collective-permute-start.6 = (bf16[512,1024]{1,0:T(8,128)(2,1)S(1)}, bf16[512,1024]{1,0:T(8,128)(2,1)}, u32[]{:S(2)}, u32[]{:S(2)}) collective-permute-start(bf16[512,1024]{1,0:T(8,128)(2,1)S(1)} %bitcast.35), channel_id=1, source_target_pairs={{0,1},{1,2},{2,3},{4,5},{5,6},{6,7},{8,9},{9,10},{10,11},{12,13},{... | collective-permute-start | bytes 3145736 | tf_op jit(solution)/shard_map/ppermute | solution.py:86
  170.8 22.1 %collective-permute-start.7 = (bf16[512,1024]{1,0:T(8,128)(2,1)S(1)}, bf16[512,1024]{1,0:T(8,128)(2,1)S(1)}, u32[]{:S(2)}, u32[]{:S(2)}) collective-permute-start(bf16[512,1024]{1,0:T(8,128)(2,1)S(1)} %bitcast.36), channel_id=1, source_target_pairs={{3,2},{2,1},{1,0},{7,6},{6,5},{5,4},{11,10},{10,9},{9,8},{15,14},{... | collective-permute-start | bytes 3145736 | tf_op jit(solution)/shard_map/ppermute | solution.py:87
  193.0 27.2 %collective-permute-start.8 = (bf16[512,1024]{1,0:T(8,128)(2,1)}, bf16[512,1024]{1,0:T(8,128)(2,1)}, u32[]{:S(2)}, u32[]{:S(2)}) collective-permute-start(bf16[512,1024]{1,0:T(8,128)(2,1)} %broadcast_select_fusion.1), channel_id=1, source_target_pairs={{0,1},{1,2},{2,3},{4,5},{5,6},{6,7},{8,9},{9,10},{10,11},{12,13},{... | collective-permute-start | bytes 3145736 | tf_op jit(solution)/shard_map/ppermute | solution.py:86
  201.0 22.3 %collective-permute-start.9 = (bf16[512,1024]{1,0:T(8,128)(2,1)S(1)}, bf16[512,1024]{1,0:T(8,128)(2,1)}, u32[]{:S(2)}, u32[]{:S(2)}) collective-permute-start(bf16[512,1024]{1,0:T(8,128)(2,1)S(1)} %broadcast_select_fusion), channel_id=1, source_target_pairs={{3,2},{2,1},{1,0},{7,6},{6,5},{5,4},{11,10},{10,9},{9,8},{15,14},{... | collective-permute-start | bytes 3145736 | tf_op jit(solution)/shard_map/ppermute | solution.py:87
  226.9 21.3 %collective-permute-start.11 = (bf16[512,1024]{1,0:T(8,128)(2,1)S(1)}, bf16[512,1024]{1,0:T(8,128)(2,1)S(1)}, u32[]{:S(2)}, u32[]{:S(2)}) collective-permute-start(bf16[512,1024]{1,0:T(8,128)(2,1)S(1)} %get-tuple-element.116), channel_id=1, source_target_pairs={{3,2},{2,1},{1,0},{7,6},{6,5},{5,4},{11,10},{10,9},{9,8},{15,14},{... | collective-permute-start | bytes 3145736 | tf_op jit(solution)/shard_map/ppermute | solution.py:87
  228.2 21.5 %collective-permute-start.10 = (bf16[512,1024]{1,0:T(8,128)(2,1)S(1)}, bf16[512,1024]{1,0:T(8,128)(2,1)S(1)}, u32[]{:S(2)}, u32[]{:S(2)}) collective-permute-start(bf16[512,1024]{1,0:T(8,128)(2,1)S(1)} %get-tuple-element.115), channel_id=1, source_target_pairs={{0,1},{1,2},{2,3},{4,5},{5,6},{6,7},{8,9},{9,10},{10,11},{12,13},{... | collective-permute-start | bytes 3145736 | tf_op jit(solution)/shard_map/ppermute | solution.py:86
  249.7 25.6 %collective-permute-start.13 = (bf16[512,1024]{1,0:T(8,128)(2,1)}, bf16[512,1024]{1,0:T(8,128)(2,1)}, u32[]{:S(2)}, u32[]{:S(2)}) collective-permute-start(bf16[512,1024]{1,0:T(8,128)(2,1)} %add_convert_fusion.7), channel_id=1, source_target_pairs={{3,2},{2,1},{1,0},{7,6},{6,5},{5,4},{11,10},{10,9},{9,8},{15,14},{... | collective-permute-start | bytes 3145736 | tf_op jit(solution)/shard_map/ppermute | solution.py:87
  252.4 22.9 %collective-permute-start.12 = (bf16[512,1024]{1,0:T(8,128)(2,1)}, bf16[512,1024]{1,0:T(8,128)(2,1)S(1)}, u32[]{:S(2)}, u32[]{:S(2)}) collective-permute-start(bf16[512,1024]{1,0:T(8,128)(2,1)} %add_convert_fusion.8), channel_id=1, source_target_pairs={{0,1},{1,2},{2,3},{4,5},{5,6},{6,7},{8,9},{9,10},{10,11},{12,13},{... | collective-permute-start | bytes 3145736 | tf_op jit(solution)/shard_map/ppermute | solution.py:86
  276.9 23.2 %collective-permute-start.14 = (bf16[1024,512]{1,0:T(8,128)(2,1)S(1)}, bf16[1024,512]{1,0:T(8,128)(2,1)S(1)}, u32[]{:S(2)}, u32[]{:S(2)}) collective-permute-start(bf16[1024,512]{1,0:T(8,128)(2,1)S(1)} %copy-done.34), channel_id=1, source_target_pairs={{0,1},{1,2},{2,3},{3,0},{4,5},{5,6},{6,7},{7,4},{8,9},{9,10},{10,1... | collective-permute-start | bytes 3145736 | tf_op jit(solution)/shard_map/ppermute | solution.py:62
  300.4 22.9 %collective-permute-start.15 = (bf16[1024,512]{1,0:T(8,128)(2,1)S(1)}, bf16[1024,512]{1,0:T(8,128)(2,1)S(1)}, u32[]{:S(2)}, u32[]{:S(2)}) collective-permute-start(bf16[1024,512]{1,0:T(8,128)(2,1)S(1)} %add_convert_fusion.6), channel_id=1, source_target_pairs={{0,1},{1,2},{2,3},{3,0},{4,5},{5,6},{6,7},{7,4},{8,9},{9,10},{10,1... | collective-permute-start | bytes 3145736 | tf_op jit(solution)/shard_map/ppermute | solution.py:62
  323.6 39.1 %collective-permute-start.16 = (bf16[1024,512]{1,0:T(8,128)(2,1)S(1)}, bf16[1024,512]{1,0:T(8,128)(2,1)}, u32[]{:S(2)}, u32[]{:S(2)}) collective-permute-start(bf16[1024,512]{1,0:T(8,128)(2,1)S(1)} %add_convert_fusion.5), channel_id=1, source_target_pairs={{0,1},{1,2},{2,3},{3,0},{4,5},{5,6},{6,7},{7,4},{8,9},{9,10},{10,1... | collective-permute-start | bytes 3145736 | tf_op jit(solution)/shard_map/ppermute | solution.py:62
  325.6 38.7 %collective-permute-start.17 = (bf16[512,1024]{1,0:T(8,128)(2,1)}, bf16[512,1024]{1,0:T(8,128)(2,1)}, u32[]{:S(2)}, u32[]{:S(2)}) collective-permute-start(bf16[512,1024]{1,0:T(8,128)(2,1)} %get-tuple-element.137), channel_id=1, source_target_pairs={{0,1},{1,2},{2,3},{3,0},{4,5},{5,6},{6,7},{7,4},{8,9},{9,10},{10,1... | collective-permute-start | bytes 3145736 | tf_op jit(solution)/shard_map/ppermute | solution.py:62
  364.3 13.5 %collective-permute-start.18 = (bf16[2048,1024]{1,0:T(8,128)(2,1)}, bf16[2048,1024]{1,0:T(8,128)(2,1)}, u32[]{:S(2)}, u32[]{:S(2)}) collective-permute-start(bf16[2048,1024]{1,0:T(8,128)(2,1)} %get-tuple-element.142), channel_id=1, source_target_pairs={{0,4},{4,0},{8,12},{12,8},{16,20},{20,16},{24,28},{28,24},{1,5},{5... | collective-permute-start | bytes 12582920 | tf_op jit(solution)/shard_map/ppermute | solution.py:110
  367.2 3.8 collective-permute-start.19
  367.4 27.9 %collective-permute-start.23 = (bf16[512,1024]{1,0:T(8,128)(2,1)}, bf16[512,1024]{1,0:T(8,128)(2,1)}, u32[]{:S(2)}, u32[]{:S(2)}) collective-permute-start(bf16[512,1024]{1,0:T(8,128)(2,1)} %add_convert_fusion.3), channel_id=1, source_target_pairs={{0,1},{1,2},{2,3},{3,0},{4,5},{5,6},{6,7},{7,4},{8,9},{9,10},{10,1... | collective-permute-start | bytes 3145736 | tf_op jit(solution)/shard_map/ppermute | solution.py:62
  371.1 3.7 collective-permute-start.20
  380.7 14.6 %collective-permute-start.22 = (f32[3072]{0:T(1024)S(1)}, f32[3072]{0:T(1024)S(1)}, u32[]{:S(2)}, u32[]{:S(2)}) collective-permute-start(f32[3072]{0:T(1024)S(1)} %pad_maximum_fusion.1), channel_id=1, source_target_pairs={{0,1},{1,0},{2,3},{3,2},{4,5},{5,4},{6,7},{7,6},{8,9},{9,8},{10,11... | collective-permute-start | bytes 36872 | tf_op jit(solution)/shard_map/ppermute | solution.py:146
  384.1 14.2 %collective-permute-start.25 = (bf16[1024,256]{1,0:T(8,128)(2,1)}, bf16[1024,256]{1,0:T(8,128)(2,1)S(1)}, u32[]{:S(2)}, u32[]{:S(2)}) collective-permute-start(bf16[1024,256]{1,0:T(8,128)(2,1)} %get-tuple-element.202), channel_id=1, source_target_pairs={{0,16},{4,20},{8,24},{12,28},{16,0},{20,4},{24,8},{28,12},{1,17},{... | collective-permute-start | bytes 1572872 | tf_op jit(solution)/shard_map/ppermute | solution.py:110
  384.2 14.1 %collective-permute-start.27 = (bf16[1024,256]{1,0:T(8,128)(2,1)}, bf16[1024,256]{1,0:T(8,128)(2,1)S(1)}, u32[]{:S(2)}, u32[]{:S(2)}) collective-permute-start(bf16[1024,256]{1,0:T(8,128)(2,1)} %get-tuple-element.203), channel_id=1, source_target_pairs={{0,8},{4,12},{8,0},{12,4},{16,24},{20,28},{24,16},{28,20},{1,9},{5... | collective-permute-start | bytes 1572872 | tf_op jit(solution)/shard_map/ppermute | solution.py:110
  398.2 27.5 %collective-permute-start.24 = (bf16[512,1024]{1,0:T(8,128)(2,1)}, bf16[512,1024]{1,0:T(8,128)(2,1)}, u32[]{:S(2)}, u32[]{:S(2)}) collective-permute-start(bf16[512,1024]{1,0:T(8,128)(2,1)} %add_convert_fusion.2), channel_id=1, source_target_pairs={{0,1},{1,2},{2,3},{3,0},{4,5},{5,6},{6,7},{7,4},{8,9},{9,10},{10,1... | collective-permute-start | bytes 3145736 | tf_op jit(solution)/shard_map/ppermute | solution.py:62
  402.6 26.0 %collective-permute-start.26 = (bf16[2048,256]{1,0:T(8,128)(2,1)}, bf16[2048,256]{1,0:T(8,128)(2,1)}, u32[]{:S(2)}, u32[]{:S(2)}) collective-permute-start(bf16[2048,256]{1,0:T(8,128)(2,1)} %get-tuple-element.152), channel_id=1, source_target_pairs={{0,8},{4,12},{8,0},{12,4},{16,24},{20,28},{24,16},{28,20},{1,9},{5... | collective-permute-start | bytes 3145736 | tf_op jit(solution)/shard_map/ppermute | solution.py:110
  402.9 25.7 %collective-permute-start.28 = (bf16[2048,256]{1,0:T(8,128)(2,1)}, bf16[2048,256]{1,0:T(8,128)(2,1)}, u32[]{:S(2)}, u32[]{:S(2)}) collective-permute-start(bf16[2048,256]{1,0:T(8,128)(2,1)} %get-tuple-element.153), channel_id=1, source_target_pairs={{0,16},{4,20},{8,24},{12,28},{16,0},{20,4},{24,8},{28,12},{1,17},{... | collective-permute-start | bytes 3145736 | tf_op jit(solution)/shard_map/ppermute | solution.py:110
  405.7 27.1 %collective-permute-start.29 = (f32[3072]{0:T(1024)S(1)}, f32[3072]{0:T(1024)S(1)}, u32[]{:S(2)}, u32[]{:S(2)}) collective-permute-start(f32[3072]{0:T(1024)S(1)} %fusion.12), channel_id=1, source_target_pairs={{0,2},{1,3},{2,0},{3,1},{4,6},{5,7},{6,4},{7,5},{8,10},{9,11},{10,... | collective-permute-start | bytes 36872 | tf_op jit(solution)/shard_map/ppermute | solution.py:146
  (38 other events, 438.7 us)
Sparse Core Ops, SparseCore 0:
  9.9 58.7 all-gather.2
  70.6 55.9 all-gather.4
  275.5 71.7 reduce-scatter.1
where the time goes:
time: 451 us; the launch traced here: 442 us
  Pallas kernels  211 us (47%)
  waiting for transfers between devices  94.2 us (21%)
  other arithmetic  52.1 us (12%)
  starting transfers between devices  46 us (10%)
  between operations  14.9 us (3%)
  local copies, waits for them, and re-layouts  13.3 us (3%)
  blocking collectives  10.2 us (2%)
    pallas_call x6, Pallas kernels, call(): pl.pallas_call(kernel, name=name, grid=(tokens // tile,), in_specs=ins, o...  89.1 us
    pallas_call x3, Pallas kernels, weight_grad(): pl.pallas_call(functools.partial(drop_first, functools.partial(weight_gra...  45 us
    ppermute x6, waiting for transfers between devices, step(): lax.ppermute(after(self.arrays[-1], gate), 'col', pairs)  42.2 us
    pallas_call x1, Pallas kernels, back_work(): pl.pallas_call(functools.partial(back_kernel, len(pack_shards), pack_tabl...  35.4 us
    ppermute x6, waiting for transfers between devices, step(): self.moving = lax.ppermute(self.sent, 'col', pairs)  26.2 us
    pallas_call x1, Pallas kernels, attention_back_work(): pl.pallas_call(functools.partial(attention_back_kernel, heads), name='att...  23.9 us
    ppermute x4, starting transfers between devices, step(): self.upward.append(lax.ppermute(up, 'col', [(0, 1), (1, 2), (2, 3)]))  21.6 us
    pallas_call x2, Pallas kernels, attention_work(): pl.pallas_call(attention_kernel, name='attention', grid=(1,), in_specs=[p...  18.1 us
  transfers between devices with their start and end apart: 33, of which 17 were waited for; matrix products, arithmetic and copies ran while one was open for 13% of the time, Pallas kernels for 48%

commit v1 on v0

--- a/solution.py
+++ b/solution.py
@@ -96,44 +96,6 @@
 
     def result(self, gate):
         return after(self.chunks[0], gate) + (self.upward[4].astype(F32) + self.downward[4].astype(F32))
-
-
-class RowScatter:
-    KEPT, SENT = [0, 2, 4, 6], [1, 3, 5, 7]
-
-    def __init__(self, kept, sent):
-        self.kept, self.sent, self.done = kept, sent, 0
-        self.width, self.parts = kept.shape[1] // 4, []
-
-    def send(self, array, mask, gate):
-        self.parts.append(after(array, gate))
-        return lax.ppermute(self.parts[-1], "row", [(k, k ^ mask) for k in range(8)])
-
-    def piece(self, at):
-        columns = slice(at * self.width, (at + 1) * self.width)
-        return self.kept[:, columns].astype(F32) + self.core[:, columns].astype(F32)
-
-    def step(self, gate):
-        self.done += 1
-        half = self.kept.shape[0] // 2
-        if self.done == 1:
-            self.core = self.send(self.sent, 1, gate)
-            return [self.core]
-        if self.done == 2:
-            far = self.piece(3).astype(BF)
-            self.from_x = self.send(far[:half], 2, gate)
-            self.from_y = self.send(far[half:], 4, gate)
-        else:
-            empty = jnp.zeros_like(self.from_x, F32)
-            from_x, from_y = self.from_x.astype(F32), self.from_y.astype(F32)
-            for_x = self.piece(1) + jnp.concatenate([empty, from_y])
-            for_y = self.piece(2) + jnp.concatenate([from_x, empty])
-            self.from_x = self.send(for_x.astype(BF), 2, gate)
-            self.from_y = self.send(for_y.astype(BF), 4, gate)
-        return [self.from_x, self.from_y]
-
-    def result(self):
-        return self.piece(0) + self.from_x.astype(F32) + self.from_y.astype(F32)
 
 
 def pair_sum(value, axis, count, masks, gate):
@@ -427,11 +389,10 @@
                 begin += width
 
 
-def back_kernel(pack_count, pack_table, up_table, pieces, *refs):
-    act, params, project, expand, *shards = refs[: -8 - len(pieces)]
+def back_kernel(pack_count, pack_table, up_table, *refs):
+    act, params, project, expand, *shards = refs[:-8]
     project_shards, up_shards = shards[:pack_count], shards[pack_count:]
-    outs = refs[-8 - len(pieces) : -8]
-    gains, project_bias, up_bias, project_whole, up_whole, project_sems, up_sems, tile = refs[-8:]
+    out, gains, project_bias, up_bias, project_whole, up_whole, project_sems, up_sems = refs[-8:]
 
     @pl.when(pl.program_id(0) == 0)
     def _():
@@ -454,16 +415,7 @@
     normed_grad = first * params[0:1, :] + second * params[2:3, :]
     mean_grad = jnp.mean(normed_grad, axis=1, keepdims=True)
     mean_product = jnp.mean(normed_grad * normed, axis=1, keepdims=True)
-    result = (inverse_scale * (normed_grad - mean_grad - normed * mean_product)).astype(BF)
-    if pieces == [None]:
-        outs[0][...] = result
-        return
-    tile[...] = result
-    place, width = lax.axis_index("row"), tile.shape[1] // 8
-    for out, masks in zip(outs, pieces):
-        for at, mask in enumerate(masks):
-            source = pl.ds(pl.multiple_of((place ^ mask) * width, width), width)
-            out[:, at * width : (at + 1) * width] = tile[:, source]
+    out[...] = (inverse_scale * (normed_grad - mean_grad - normed * mean_product)).astype(BF)
 
 
 def tile_spec(width, tile=TILE):
@@ -809,35 +761,28 @@
             tile=2 * TILE,
         )
 
-    pieces = [RowScatter.KEPT, RowScatter.SENT] if rows == 8 else [None]
-
     def back_work(gate):
-        widths = project_width, hidden_width
-        share = D // len(pieces)
-        return pl.pallas_call(
-            functools.partial(back_kernel, len(pack_shards), pack_table, up_table, pieces),
-            name="back",
-            grid=(tokens // TILE,),
-            in_specs=[tile_spec(D), fixed_spec((4, D)), *map(tile_spec, widths)]
+        return call(
+            functools.partial(back_kernel, len(pack_shards), pack_table, up_table),
+            "back",
+            tokens,
+            [tile_spec(D), fixed_spec((4, D)), tile_spec(project_width), tile_spec(hidden_width)]
             + [ANY] * (len(pack_shards) + len(up_shards)),
-            out_specs=[tile_spec(share)] * len(pieces)
-            + [fixed_spec((4, D)), *[fixed_spec((1, width)) for width in widths]],
-            out_shape=[shape_of((tokens, share), BF)] * len(pieces)
-            + [shape_of((4, D), F32), *[shape_of((1, width), F32) for width in widths]],
-            scratch_shapes=[pltpu.VMEM((D, width), BF) for width in widths]
-            + [pltpu.SemaphoreType.DMA((cols,))] * 2
-            + [pltpu.VMEM((TILE, D), BF)],
-            compiler_params=pltpu.CompilerParams(
-                dimension_semantics=("arbitrary",), vmem_limit_bytes=VMEM_LIMIT
-            ),
-            cost_estimate=cost(2 * tokens * D * sum(widths)),
-        )(
-            full_input,
-            norm_params,
-            project_grad,
-            after(expand_grad, gate),
-            *pack_shards,
-            *up_shards,
+            [
+                (tile_spec(D), shape_of((tokens, D), BF)),
+                (fixed_spec((4, D)), shape_of((4, D), F32)),
+                (fixed_spec((1, project_width)), shape_of((1, project_width), F32)),
+                (fixed_spec((1, hidden_width)), shape_of((1, hidden_width), F32)),
+            ],
+            [((D, project_width), cols), ((D, hidden_width), cols)],
+            [
+                full_input,
+                norm_params,
+                project_grad,
+                after(expand_grad, gate),
+                *pack_shards,
+                *up_shards,
+            ],
         )
 
     def up_weight_work(gate):
@@ -855,11 +800,12 @@
     mixed_sum = lax.psum_scatter(after(mixed_part, gate), "row", scatter_dimension=1, tiled=True)
     gate, ((expand_grad,),) = slot([down_scatter], gate, hidden_grad_work)
     gate = more([down_scatter], gate)
+    gate, ((back_part, gains, project_bias_grad, up_bias_grad),) = slot(
+        [down_scatter], gate, back_work
+    )
+    back_sum = lax.psum_scatter(after(back_part, gate), "row", scatter_dimension=1, tiled=True)
     gate, (up_chunks,) = slot([down_scatter], gate, up_weight_work)
     up_scatter = RingScatter(up_chunks, cols)
-    gate, ((*back_parts, gains, project_bias_grad, up_bias_grad),) = slot(
-        [down_scatter, up_scatter], gate, back_work
-    )
 
     def split_work(gate):
         parts = pack_scatter.result(gate)
@@ -871,33 +817,20 @@
         terms = terms.reshape(4, rows, features).transpose(1, 0, 2).reshape(rows, -1)
         return [pair_scatter(terms, "row", rows, row_place)]
 
-    row_scatter = RowScatter(*back_parts) if rows == 8 else None
-    row_steps = [row_scatter] if rows == 8 else []
-
-    for step in row_steps + [up_scatter]:
-        step.step(gate)
+    up_scatter.step(gate)
     (gain_terms,) = gains_work(gate + [up_scatter.sent])
     (down_weight_grad,) = down_result_work(gate)
     project_weight_grad, output_weight_grad = split_work(gate)
-    for step in row_steps:
-        step.step([])
+    up_scatter.step([down_weight_grad, project_weight_grad, output_weight_grad, gain_terms])
     small = [gain_terms, project_bias_grad[0], up_bias_grad[0], shift_out_grad]
     masks = [1 << bit for bit in range(cols.bit_length() - 1)]
-    gate = row_scatter.parts if row_scatter is not None else []
-    small = pair_sum(jnp.concatenate(small), "col", cols, masks[:-1], gate)
-    gate = gate + [down_weight_grad, project_weight_grad, output_weight_grad, small]
+    small = pair_sum(jnp.concatenate(small), "col", cols, masks[:-1], [up_scatter.sent])
     for _ in range(cols - 3):
-        up_scatter.step(gate)
+        up_scatter.step([small])
     (layer_out,) = layer_out_work([up_scatter.sent])
     arrived = pair_exchange(small, "col", cols, masks[-1], [up_scatter.sent])
-    for step in row_steps:
-        step.step([up_scatter.sent])
-    up_weight_grad = up_scatter.result([layer_out])
-    if row_scatter is not None:
-        back_sum = row_scatter.result()
-    else:
-        back_sum = lax.psum_scatter(back_parts[0], "row", scatter_dimension=1, tiled=True)
-    activations_grad = after(out_grad, [up_weight_grad]).astype(F32) + back_sum.astype(F32)
+    activations_grad = after(out_grad, [layer_out]).astype(F32) + back_sum.astype(F32)
+    up_weight_grad = up_scatter.result([activations_grad])
     small = after(small, [activations_grad]) + arrived
     sizes = [features] * 4 + [project_width, hidden_width, features]
     pieces, begin = [], 0

time: 451 us -> 451 us (level)
  the two profiles are of different devices: /device:TPU:0 before, /device:TPU:5 now
where the time goes in v1:
time: 451 us; the launch traced here: 442 us
  Pallas kernels  207 us (46%)
  waiting for transfers between devices  91.7 us (20%)
  starting transfers between devices  59.5 us (13%)
  other arithmetic  44.4 us (10%)
  between operations  14.8 us (3%)
  local copies, waits for them, and re-layouts  13.4 us (3%)
  blocking collectives  11.4 us (3%)
    pallas_call x7, Pallas kernels, call(): pl.pallas_call(kernel, name=name, grid=(tokens // tile,), in_specs=ins, o...  123 us
    pallas_call x3, Pallas kernels, weight_grad(): pl.pallas_call(functools.partial(drop_first, functools.partial(weight_gra...  45.2 us
    ppermute x6, waiting for transfers between devices, step(): lax.ppermute(after(self.arrays[-1], gate), 'col', pairs)  32.8 us
    ppermute x2, waiting for transfers between devices, pair_exchange(): lax.ppermute(after(value, gate), axis, [(k, k ^ mask) for k in range(coun...  25.8 us
    ppermute x3, starting transfers between devices, pair_scatter(): lax.ppermute(sent, axis, [(k, k ^ mask) for k in range(count)])  23.6 us
    pallas_call x1, Pallas kernels, attention_back_work(): pl.pallas_call(functools.partial(attention_back_kernel, heads), name='att...  22.4 us
    ppermute x4, starting transfers between devices, step(): self.upward.append(lax.ppermute(up, 'col', [(0, 1), (1, 2), (2, 3)]))  17.1 us
    pallas_call x2, Pallas kernels, attention_work(): pl.pallas_call(attention_kernel, name='attention', grid=(1,), in_specs=[p...  16.7 us
  transfers between devices with their start and end apart: 29, of which 13 were waited for; matrix products, arithmetic and copies ran while one was open for 11% of the time, Pallas kernels for 47%

profile of v1, /device:TPU:5, one launch (start us, length us, event | category | flops | bytes accessed | tf_op | source)
XLA Modules:
  0.0 442.0 jit_solution(12002044933928391198)
XLA Ops:
  14.0 5.4 %multiply_sine_fusion = (f32[2048,16]{1,0:T(8,128)S(1)}, f32[2048,16]{1,0:T(8,128)}, f32[2048,16]{1,0:T(8,128)S(1)}) fusion(f32[2048]{0:T(1024)S(1)} %fusion.5, f32[16]{0:T(128)S(1)} %multiply_power_fusion), kind=kLoop, calls=%fused_computation.19 | loop fusion | flops 65536 | bytes 401472 | tf_op jit(solution)/shard_map/sin | solution.py:498
  28.6 8.6 %collective-permute-done.refs_6_.refs_2_.refs_3_.refs_5_ = bf16[512,1024]{1,0:T(8,128)(2,1)} collective-permute-done((bf16[512,1024]{1,0:T(8,128)(2,1)}, bf16[512,1024]{1,0:T(8,128)(2,1)}, u32[]{:S(2)}, u32[]{:S(2)}) %collective-permute-start) | collective-permute-done | bytes 1048608 | tf_op jit(solution)/shard_map/ppermute | solution.py:41
  37.3 11.4 %all_gather.10.params.refs_1_ = f32[4,2048]{1,0:T(4,128)} all-gather(f32[4,256]{1,0:T(4,128)S(1)} %pad_maximum_fusion.2), channel_id=1, replica_groups=mesh['row'=8,'col'=4] {'row'}, dimensions={1}, use_global_device_ids=true | all-gather | bytes 36864 | tf_op jit(solution)/shard_map/all_gather | solution.py:570
  48.7 13.8 %collective-permute-done.1.refs_7_.refs_3_.refs_4_.refs_6_ = bf16[512,1024]{1,0:T(8,128)(2,1)S(1)} collective-permute-done((bf16[512,1024]{1,0:T(8,128)(2,1)}, bf16[512,1024]{1,0:T(8,128)(2,1)S(1)}, u32[]{:S(2)}, u32[]{:S(2)}) %collective-permute-start.1) | collective-permute-done | bytes 1048608 | tf_op jit(solution)/shard_map/ppermute | solution.py:41
  62.6 3.8 all-gather.3.cloned.1.call-done.act.refs_0_
  66.5 14.0 %norm.1 = (bf16[2048,2048]{1,0:T(8,128)(2,1)}, bf16[2048,2048]{1,0:T(8,128)(2,1)}) custom-call(bf16[2048,2048]{1,0:T(8,128)(2,1)} %all-gather.3.cloned.1.call-done.act.refs_0_, f32[4,2048]{1,0:T(4,128)} %all_gather.10.params.refs_1_), custom_call_target="tpu_custom_call" | custom-call | bytes 25165824 | tf_op jit(solution)/shard_map/norm/pallas_call | solution.py:444
  80.5 6.1 %collective-permute-done.2.refs_8_.refs_4_.refs_5_.refs_7_ = bf16[512,1024]{1,0:T(8,128)(2,1)} collective-permute-done((bf16[512,1024]{1,0:T(8,128)(2,1)S(1)}, bf16[512,1024]{1,0:T(8,128)(2,1)}, u32[]{:S(2)}, u32[]{:S(2)}) %collective-permute-start.2) | collective-permute-done | bytes 1048608 | tf_op jit(solution)/shard_map/ppermute | solution.py:41
  87.7 14.5 %project.1 = bf16[2048,768]{1,0:T(8,128)(2,1)} custom-call(bf16[2048,2048]{1,0:T(8,128)(2,1)} %get-tuple-element.88.refs_0_, f32[1,768]{1,0:T(1,128)} %bitcast.47, f32[2048,128]{1,0:T(8,128)} %maximum_maximum_fusion.refs_2_.cosine, f32[2048,128]{1,0:T(8,128)} %get-tuple-element.193.refs_3_.left, f32[2048,128]{1,0:T(8,128)} %get-tuple-element.192.refs_4_.right, ...), custom_call_target="tpu_custom_call" | custom-call | flops 6442450944 | tf_op jit(solution)/shard_map/project/pallas_call | solution.py:444
  102.2 8.3 %attention.2 = (bf16[2048,256]{1,0:T(8,128)(2,1)}, f32[128,2048]{1,0:T(8,128)}, f32[1,2048]{1,0:T(1,128)}) custom-call(s32[4]{0:T(128)} %get-tuple-element.207.low, s32[4]{0:T(128)} %get-tuple-element.206.high, s32[1,2048]{1,0:T(1,128)} %bitcast.53, bf16[2048,768]{1,0:T(8,128)(2,1)} %project.1), custom_call_target="tpu_custom_call" | custom-call | flops 4294967296 | tf_op jit(solution)/shard_map/attention/pallas_call | solution.py:634
  110.9 8.4 %attention.3 = (bf16[2048,256]{1,0:T(8,128)(2,1)}, f32[128,2048]{1,0:T(8,128)}, f32[1,2048]{1,0:T(1,128)}) custom-call(s32[4]{0:T(128)} %get-tuple-element.207.low, s32[4]{0:T(128)} %get-tuple-element.206.high, s32[1,2048]{1,0:T(1,128)} %bitcast.54, bf16[2048,768]{1,0:T(8,128)(2,1)} %project.1, ...), custom_call_target="tpu_custom_call", output_to_operand_aliasing={{0}: (4, {})} | custom-call | flops 4294967296 | tf_op jit(solution)/shard_map/attention/pallas_call | solution.py:634
  119.3 5.1 %all-gather.5.cloned.1.call-done.refs_0_.refs_2_.refs_1_ = bf16[2048,2048]{1,0:T(8,128)(2,1)} async-done(((bf16[2048,256]{1,0:T(8,128)(2,1)}), bf16[2048,2048]{1,0:T(8,128)(2,1)}) %all-gather.5.cloned.1.call-update) | async-done | bytes 8388624 | tf_op jit(solution)/shard_map/all_gather | solution.py:534
  124.3 7.2 %attended_grad.1.grad = bf16[2048,256]{1,0:T(8,128)(2,1)} custom-call(bf16[2048,2048]{1,0:T(8,128)(2,1)} %all-gather.5.cloned.1.call-done.refs_0_.refs_2_.refs_1_, bf16[512,1024]{1,0:T(8,128)(2,1)} %pad_maximum_fusion.refs_5_.refs_1_.refs_2_.refs_4_, bf16[512,1024]{1,0:T(8,128)(2,1)} %collective-permute-done.refs_6_.refs_2_.refs_3_.refs_5_, ...), custom_call_target="tpu_custom_call" | custom-call | flops 2147483648 | tf_op jit(solution)/shard_map/attended_grad/pallas_call | solution.py:444
  131.5 4.4 collective-permute-done.4.refs_4_.refs_10_
  135.9 22.4 %attention_back.1.refs_1_.refs_2_ = bf16[2048,768]{1,0:T(8,128)(2,1)} custom-call(s32[4]{0:T(128)} %get-tuple-element.207.low, s32[4]{0:T(128)} %get-tuple-element.206.high, s32[1,2048]{1,0:T(1,128)} %bitcast.55, f32[2048,128]{1,0:T(8,128)} %maximum_maximum_fusion.refs_2_.cosine, f32[2048,128]{1,0:T(8,128)} %get-tuple-element.193.refs_3_.left, ...), custom_call_target="tpu_custom_call" | custom-call | flops 17179869184 | tf_op jit(solution)/shard_map/attention_back/pallas_call | solution.py:654
  163.2 15.4 %weight_grad.3 = (f32[512,1024]{1,0:T(8,128)}, bf16[512,1024]{1,0:T(8,128)(2,1)}, bf16[512,1024]{1,0:T(8,128)(2,1)}, bf16[512,1024]{1,0:T(8,128)(2,1)}) custom-call(s32[1]{0:T(128)} %bitcast.7.spot, bf16[2048,2048]{1,0:T(8,128)(2,1)} %get-tuple-element.88.refs_0_, bf16[2048,768]{1,0:T(8,128)(2,1)} %attention_back.1.refs_1_.refs_2_, ...), custom_call_target="tpu_custom_call" | custom-call | flops 8589934592 | tf_op jit(solution)/shard_map/weight_grad/pallas_call | solution.py:473
  181.0 4.6 %collective-permute-done.7.refs_10_.refs_6_ = bf16[512,1024]{1,0:T(8,128)(2,1)S(1)} collective-permute-done((bf16[512,1024]{1,0:T(8,128)(2,1)S(1)}, bf16[512,1024]{1,0:T(8,128)(2,1)S(1)}, u32[]{:S(2)}, u32[]{:S(2)}) %collective-permute-start.7) | collective-permute-done | bytes 1048608 | tf_op jit(solution)/shard_map/ppermute | solution.py:87
  185.7 5.5 %collective-permute-start.8 = (bf16[512,1024]{1,0:T(8,128)(2,1)}, bf16[512,1024]{1,0:T(8,128)(2,1)}, u32[]{:S(2)}, u32[]{:S(2)}) collective-permute-start(bf16[512,1024]{1,0:T(8,128)(2,1)} %broadcast_select_fusion.1), channel_id=1, source_target_pairs={{0,1},{1,2},{2,3},{4,5},{5,6},{6,7},{8,9},{9,10},{10,11},{12,13},{... | collective-permute-start | bytes 3145736 | tf_op jit(solution)/shard_map/ppermute | solution.py:86
  192.6 17.8 %up.1 = (bf16[2048,1024]{1,0:T(8,128)(2,1)}, f32[2048,1024]{1,0:T(8,128)}) custom-call(bf16[2048,2048]{1,0:T(8,128)(2,1)} %get-tuple-element.109.refs_0_, f32[1,1024]{1,0:T(1,128)} %bitcast.52, bf16[512,1024]{1,0:T(8,128)(2,1)} %convert_element_type.146.refs_2_.refs_8_, bf16[512,1024]{1,0:T(8,128)(2,1)} %copy-done.31, bf16[512,1024]{1,0:T(8,128)(2,1)} %copy-done.32, ...), custom_call_target="tpu_custom_call" | custom-call | flops 8589934592 | tf_op jit(solution)/shard_map/up/pallas_call | solution.py:444
  211.1 3.6 fusion.2
  216.0 5.3 %collective-permute-start.10 = (bf16[512,1024]{1,0:T(8,128)(2,1)S(1)}, bf16[512,1024]{1,0:T(8,128)(2,1)S(1)}, u32[]{:S(2)}, u32[]{:S(2)}) collective-permute-start(bf16[512,1024]{1,0:T(8,128)(2,1)S(1)} %get-tuple-element.112), channel_id=1, source_target_pairs={{0,1},{1,2},{2,3},{4,5},{5,6},{6,7},{8,9},{9,10},{10,11},{12,13},{... | collective-permute-start | bytes 3145736 | tf_op jit(solution)/shard_map/ppermute | solution.py:86
  221.3 14.8 %weight_grad.4 = (f32[1024,512]{1,0:T(8,128)}, bf16[1024,512]{1,0:T(8,128)(2,1)}, bf16[1024,512]{1,0:T(8,128)(2,1)}, bf16[1024,512]{1,0:T(8,128)(2,1)}) custom-call(s32[1]{0:T(128)} %bitcast.7.spot, bf16[2048,1024]{1,0:T(8,128)(2,1)} %get-tuple-element.114.refs_0_.refs_1_, bf16[2048,2048]{1,0:T(8,128)(2,1)} %all-gather.5.cloned.1.call-done.refs_0_.refs_2_.refs_1_), custom_call_target="tpu_custom_call" | custom-call | flops 8589934592 | tf_op jit(solution)/shard_map/weight_grad/pallas_call | solution.py:473
  240.2 4.0 collective-permute-start.12
  244.3 17.9 %mixed.1 = bf16[2048,2048]{1,0:T(8,128)(2,1)} custom-call(bf16[2048,256]{1,0:T(8,128)(2,1)} %get-tuple-element.119.refs_3_.refs_0_, bf16[2048,1024]{1,0:T(8,128)(2,1)} %get-tuple-element.114.refs_0_.refs_1_, bf16[512,1024]{1,0:T(8,128)(2,1)} %pad_maximum_fusion.refs_5_.refs_1_.refs_2_.refs_4_, ...), custom_call_target="tpu_custom_call" | custom-call | flops 10737418240 | tf_op jit(solution)/shard_map/mixed/pallas_call | solution.py:444
  265.3 15.5 %hidden_grad.1.refs_3_.refs_1_ = bf16[2048,1024]{1,0:T(8,128)(2,1)} custom-call(bf16[2048,2048]{1,0:T(8,128)(2,1)} %all-gather.5.cloned.1.call-done.refs_0_.refs_2_.refs_1_, f32[2048,1024]{1,0:T(8,128)} %get-tuple-element.111.refs_1_, bf16[512,1024]{1,0:T(8,128)(2,1)} %bitcast.34, bf16[512,1024]{1,0:T(8,128)(2,1)} %collective-permute-done.6.refs_7_.refs_3_, ...), custom_call_target="tpu_custom_call" | custom-call | flops 8589934592 | tf_op jit(solution)/shard_map/hidden_grad/pallas_call | solution.py:444
  285.2 35.5 %back.1 = (bf16[2048,2048]{1,0:T(8,128)(2,1)}, f32[4,2048]{1,0:T(4,128)}, f32[1,768]{1,0:T(1,128)}, f32[1,1024]{1,0:T(1,128)}) custom-call(bf16[2048,2048]{1,0:T(8,128)(2,1)} %all-gather.3.cloned.1.call-done.act.refs_0_, f32[4,2048]{1,0:T(4,128)} %all_gather.10.params.refs_1_, bf16[2048,768]{1,0:T(8,128)(2,1)} %attention_back.1.refs_1_.refs_2_, ...), custom_call_target="tpu_custom_call" | custom-call | flops 15032385536 | tf_op jit(solution)/shard_map/back/pallas_call | solution.py:444
  324.3 15.0 %weight_grad.5 = (f32[512,1024]{1,0:T(8,128)}, bf16[512,1024]{1,0:T(8,128)(2,1)}, bf16[512,1024]{1,0:T(8,128)(2,1)}, bf16[512,1024]{1,0:T(8,128)(2,1)}) custom-call(s32[1]{0:T(128)} %bitcast.7.spot, bf16[2048,2048]{1,0:T(8,128)(2,1)} %get-tuple-element.109.refs_0_, bf16[2048,1024]{1,0:T(8,128)(2,1)} %hidden_grad.1.refs_3_.refs_1_), custom_call_target="tpu_custom_call" | custom-call | flops 8589934592 | tf_op jit(solution)/shard_map/weight_grad/pallas_call | solution.py:473
  341.4 3.0 collective-permute-start.17
  349.5 20.5 %collective-permute-start.19 = (f32[1,1024]{1,0:T(1,128)S(1)}, f32[1,1024]{1,0:T(1,128)S(1)}, u32[]{:S(2)}, u32[]{:S(2)}) collective-permute-start(f32[1,1024]{1,0:T(1,128)S(1)} %broadcast_select_fusion.3), channel_id=1, source_target_pairs={{0,4},{4,0},{8,12},{12,8},{16,20},{20,16},{24,28},{28,24},{1,5},{5... | collective-permute-start | bytes 12296 | tf_op jit(solution)/shard_map/ppermute | solution.py:117
  378.6 20.7 %collective-permute-done.21 = f32[3072]{0:T(1024)S(1)} collective-permute-done((f32[3072]{0:T(1024)S(1)}, f32[3072]{0:T(1024)S(1)}, u32[]{:S(2)}, u32[]{:S(2)}) %collective-permute-start.21) | collective-permute-done | bytes 12320 | tf_op jit(solution)/shard_map/ppermute | solution.py:108
  399.4 2.9 add_convert_fusion
  407.5 14.5 %reduce-scatter.5.cloned.1.call-done = bf16[2048,256]{1,0:T(8,128)(2,1)} async-done(((bf16[2048,2048]{1,0:T(8,128)(2,1)}), bf16[2048,256]{1,0:T(8,128)(2,1)}) %reduce-scatter.5.cloned.1.call-update) | async-done | bytes 1048592 | tf_op jit(solution)/shard_map/reduce_scatter | solution.py:806
  424.8 5.1 %collective-permute-done.23 = f32[3072]{0:T(1024)S(1)} collective-permute-done((f32[3072]{0:T(1024)S(1)}, f32[3072]{0:T(1024)S(1)}, u32[]{:S(2)}, u32[]{:S(2)}) %collective-permute-start.23) | collective-permute-done | bytes 12320 | tf_op jit(solution)/shard_map/ppermute | solution.py:108
  (175 shorter events, 72.1 us)
Async XLA Ops:
  7.2 59.3 %all-gather.3.cloned.1.call-start = ((), (), s32[]{:S(2)}) async-start(), calls=%async_computation.2 | async-start | bytes 9437184 | tf_op jit(solution)/shard_map/all_gather | solution.py:533
  7.9 116.4 %all-gather.5.cloned.1.call-start = ((), (), s32[]{:S(2)}) async-start(), calls=%async_computation.3 | async-start | bytes 9437184 | tf_op jit(solution)/shard_map/all_gather | solution.py:534
  8.7 395.9 %reduce-scatter.3.cloned.1.call-start = ((), (), s32[]{:S(2)}) async-start(), calls=%async_computation.4 | async-start | bytes 9437184 | tf_op jit(solution)/shard_map/reduce_scatter | solution.py:800
  11.0 26.3 %collective-permute-start = (bf16[512,1024]{1,0:T(8,128)(2,1)}, bf16[512,1024]{1,0:T(8,128)(2,1)}, u32[]{:S(2)}, u32[]{:S(2)}) collective-permute-start(bf16[512,1024]{1,0:T(8,128)(2,1)} %pad_maximum_fusion.refs_5_.refs_1_.refs_2_.refs_4_), channel_id=1, source_target_pairs={{0,1},{1,2},{2,3},{3,0},{4,5},{5,6},{6,7},{7,4},{8,9},{9,10},{10,1... | collective-permute-start | bytes 3145736 | tf_op jit(solution)/shard_map/ppermute | solution.py:41
  14.0 48.5 %copy-start.36 = (s32[2048]{0:T(1024)}, s32[2048]{0:T(1024)S(1)}, u32[]{:S(2)}) copy-start(s32[2048]{0:T(1024)S(1)} %convert_reduce_fusion) | copy-start | bytes 24580
  37.2 25.2 %collective-permute-start.1 = (bf16[512,1024]{1,0:T(8,128)(2,1)}, bf16[512,1024]{1,0:T(8,128)(2,1)S(1)}, u32[]{:S(2)}, u32[]{:S(2)}) collective-permute-start(bf16[512,1024]{1,0:T(8,128)(2,1)} %collective-permute-done.refs_6_.refs_2_.refs_3_.refs_5_), channel_id=1, source_target_pairs={{0,1},{1,2},{2,3},{3,0},{4,5},{5,6},{6,7},{7,4},{8,9},{9,10},{10,1... | collective-permute-start | bytes 3145736 | tf_op jit(solution)/shard_map/ppermute | solution.py:41
  62.4 24.2 %collective-permute-start.2 = (bf16[512,1024]{1,0:T(8,128)(2,1)S(1)}, bf16[512,1024]{1,0:T(8,128)(2,1)}, u32[]{:S(2)}, u32[]{:S(2)}) collective-permute-start(bf16[512,1024]{1,0:T(8,128)(2,1)S(1)} %collective-permute-done.1.refs_7_.refs_3_.refs_4_.refs_6_), channel_id=1, source_target_pairs={{0,1},{1,2},{2,3},{3,0},{4,5},{5,6},{6,7},{7,4},{8,9},{9,10},{10,1... | collective-permute-start | bytes 3145736 | tf_op jit(solution)/shard_map/ppermute | solution.py:41
  86.6 24.0 %collective-permute-start.3 = (bf16[512,1024]{1,0:T(8,128)(2,1)S(1)}, bf16[512,1024]{1,0:T(8,128)(2,1)S(1)}, u32[]{:S(2)}, u32[]{:S(2)}) collective-permute-start(bf16[512,1024]{1,0:T(8,128)(2,1)S(1)} %copy-done.9), channel_id=1, source_target_pairs={{0,1},{1,2},{2,3},{3,0},{4,5},{5,6},{6,7},{7,4},{8,9},{9,10},{10,1... | collective-permute-start | bytes 3145736 | tf_op jit(solution)/shard_map/ppermute | solution.py:41
  110.6 25.3 %collective-permute-start.4 = (bf16[512,1024]{1,0:T(8,128)(2,1)S(1)}, bf16[512,1024]{1,0:T(8,128)(2,1)S(1)}, u32[]{:S(2)}, u32[]{:S(2)}) collective-permute-start(bf16[512,1024]{1,0:T(8,128)(2,1)S(1)} %collective-permute-done.3.refs_3_.refs_9_), channel_id=1, source_target_pairs={{0,1},{1,2},{2,3},{3,0},{4,5},{5,6},{6,7},{7,4},{8,9},{9,10},{10,1... | collective-permute-start | bytes 3145736 | tf_op jit(solution)/shard_map/ppermute | solution.py:41
  135.9 22.4 %collective-permute-start.5 = (bf16[512,1024]{1,0:T(8,128)(2,1)S(1)}, bf16[512,1024]{1,0:T(8,128)(2,1)S(1)}, u32[]{:S(2)}, u32[]{:S(2)}) collective-permute-start(bf16[512,1024]{1,0:T(8,128)(2,1)S(1)} %collective-permute-done.4.refs_4_.refs_10_), channel_id=1, source_target_pairs={{0,1},{1,2},{2,3},{3,0},{4,5},{5,6},{6,7},{7,4},{8,9},{9,10},{10,1... | collective-permute-start | bytes 3145736 | tf_op jit(solution)/shard_map/ppermute | solution.py:41
  159.3 19.4 %collective-permute-start.6 = (bf16[512,1024]{1,0:T(8,128)(2,1)S(1)}, bf16[512,1024]{1,0:T(8,128)(2,1)}, u32[]{:S(2)}, u32[]{:S(2)}) collective-permute-start(bf16[512,1024]{1,0:T(8,128)(2,1)S(1)} %bitcast.35), channel_id=1, source_target_pairs={{0,1},{1,2},{2,3},{4,5},{5,6},{6,7},{8,9},{9,10},{10,11},{12,13},{... | collective-permute-start | bytes 3145736 | tf_op jit(solution)/shard_map/ppermute | solution.py:86
  161.5 24.1 %collective-permute-start.7 = (bf16[512,1024]{1,0:T(8,128)(2,1)S(1)}, bf16[512,1024]{1,0:T(8,128)(2,1)S(1)}, u32[]{:S(2)}, u32[]{:S(2)}) collective-permute-start(bf16[512,1024]{1,0:T(8,128)(2,1)S(1)} %bitcast.36), channel_id=1, source_target_pairs={{3,2},{2,1},{1,0},{7,6},{6,5},{5,4},{11,10},{10,9},{9,8},{15,14},{... | collective-permute-start | bytes 3145736 | tf_op jit(solution)/shard_map/ppermute | solution.py:87
  185.7 24.8 %collective-permute-start.8 = (bf16[512,1024]{1,0:T(8,128)(2,1)}, bf16[512,1024]{1,0:T(8,128)(2,1)}, u32[]{:S(2)}, u32[]{:S(2)}) collective-permute-start(bf16[512,1024]{1,0:T(8,128)(2,1)} %broadcast_select_fusion.1), channel_id=1, source_target_pairs={{0,1},{1,2},{2,3},{4,5},{5,6},{6,7},{8,9},{9,10},{10,11},{12,13},{... | collective-permute-start | bytes 3145736 | tf_op jit(solution)/shard_map/ppermute | solution.py:86
  191.3 19.8 %collective-permute-start.9 = (bf16[512,1024]{1,0:T(8,128)(2,1)S(1)}, bf16[512,1024]{1,0:T(8,128)(2,1)}, u32[]{:S(2)}, u32[]{:S(2)}) collective-permute-start(bf16[512,1024]{1,0:T(8,128)(2,1)S(1)} %broadcast_select_fusion), channel_id=1, source_target_pairs={{3,2},{2,1},{1,0},{7,6},{6,5},{5,4},{11,10},{10,9},{9,8},{15,14},{... | collective-permute-start | bytes 3145736 | tf_op jit(solution)/shard_map/ppermute | solution.py:87
  214.7 21.5 %collective-permute-start.11 = (bf16[512,1024]{1,0:T(8,128)(2,1)S(1)}, bf16[512,1024]{1,0:T(8,128)(2,1)S(1)}, u32[]{:S(2)}, u32[]{:S(2)}) collective-permute-start(bf16[512,1024]{1,0:T(8,128)(2,1)S(1)} %get-tuple-element.113), channel_id=1, source_target_pairs={{3,2},{2,1},{1,0},{7,6},{6,5},{5,4},{11,10},{10,9},{9,8},{15,14},{... | collective-permute-start | bytes 3145736 | tf_op jit(solution)/shard_map/ppermute | solution.py:87
  216.0 21.5 %collective-permute-start.10 = (bf16[512,1024]{1,0:T(8,128)(2,1)S(1)}, bf16[512,1024]{1,0:T(8,128)(2,1)S(1)}, u32[]{:S(2)}, u32[]{:S(2)}) collective-permute-start(bf16[512,1024]{1,0:T(8,128)(2,1)S(1)} %get-tuple-element.112), channel_id=1, source_target_pairs={{0,1},{1,2},{2,3},{4,5},{5,6},{6,7},{8,9},{9,10},{10,11},{12,13},{... | collective-permute-start | bytes 3145736 | tf_op jit(solution)/shard_map/ppermute | solution.py:86
  237.5 24.7 %collective-permute-start.13 = (bf16[512,1024]{1,0:T(8,128)(2,1)}, bf16[512,1024]{1,0:T(8,128)(2,1)}, u32[]{:S(2)}, u32[]{:S(2)}) collective-permute-start(bf16[512,1024]{1,0:T(8,128)(2,1)} %add_convert_fusion.4), channel_id=1, source_target_pairs={{3,2},{2,1},{1,0},{7,6},{6,5},{5,4},{11,10},{10,9},{9,8},{15,14},{... | collective-permute-start | bytes 3145736 | tf_op jit(solution)/shard_map/ppermute | solution.py:87
  240.2 22.0 %collective-permute-start.12 = (bf16[512,1024]{1,0:T(8,128)(2,1)}, bf16[512,1024]{1,0:T(8,128)(2,1)S(1)}, u32[]{:S(2)}, u32[]{:S(2)}) collective-permute-start(bf16[512,1024]{1,0:T(8,128)(2,1)} %add_convert_fusion.5), channel_id=1, source_target_pairs={{0,1},{1,2},{2,3},{4,5},{5,6},{6,7},{8,9},{9,10},{10,11},{12,13},{... | collective-permute-start | bytes 3145736 | tf_op jit(solution)/shard_map/ppermute | solution.py:86
  263.2 158.8 %reduce-scatter.5.cloned.1.call-start = ((), (), s32[]{:S(2)}) async-start(), calls=%async_computation.5 | async-start | bytes 9437184 | tf_op jit(solution)/shard_map/reduce_scatter | solution.py:806
  263.8 18.8 %collective-permute-start.14 = (bf16[1024,512]{1,0:T(8,128)(2,1)S(1)}, bf16[1024,512]{1,0:T(8,128)(2,1)S(1)}, u32[]{:S(2)}, u32[]{:S(2)}) collective-permute-start(bf16[1024,512]{1,0:T(8,128)(2,1)S(1)} %copy-done.34), channel_id=1, source_target_pairs={{0,1},{1,2},{2,3},{3,0},{4,5},{5,6},{6,7},{7,4},{8,9},{9,10},{10,1... | collective-permute-start | bytes 3145736 | tf_op jit(solution)/shard_map/ppermute | solution.py:62
  282.9 37.8 %collective-permute-start.15 = (bf16[1024,512]{1,0:T(8,128)(2,1)S(1)}, bf16[1024,512]{1,0:T(8,128)(2,1)}, u32[]{:S(2)}, u32[]{:S(2)}) collective-permute-start(bf16[1024,512]{1,0:T(8,128)(2,1)S(1)} %add_convert_fusion.3), channel_id=1, source_target_pairs={{0,1},{1,2},{2,3},{3,0},{4,5},{5,6},{6,7},{7,4},{8,9},{9,10},{10,1... | collective-permute-start | bytes 3145736 | tf_op jit(solution)/shard_map/ppermute | solution.py:62
  323.5 15.8 %collective-permute-start.16 = (bf16[1024,512]{1,0:T(8,128)(2,1)S(1)}, bf16[1024,512]{1,0:T(8,128)(2,1)S(1)}, u32[]{:S(2)}, u32[]{:S(2)}) collective-permute-start(bf16[1024,512]{1,0:T(8,128)(2,1)S(1)} %add_convert_fusion.2), channel_id=1, source_target_pairs={{0,1},{1,2},{2,3},{3,0},{4,5},{5,6},{6,7},{7,4},{8,9},{9,10},{10,1... | collective-permute-start | bytes 3145736 | tf_op jit(solution)/shard_map/ppermute | solution.py:62
  339.2 32.8 %collective-permute-start.20 = (bf16[512,1024]{1,0:T(8,128)(2,1)}, bf16[512,1024]{1,0:T(8,128)(2,1)}, u32[]{:S(2)}, u32[]{:S(2)}) collective-permute-start(bf16[512,1024]{1,0:T(8,128)(2,1)} %get-tuple-element.137), channel_id=1, source_target_pairs={{0,1},{1,2},{2,3},{3,0},{4,5},{5,6},{6,7},{7,4},{8,9},{9,10},{10,1... | collective-permute-start | bytes 3145736 | tf_op jit(solution)/shard_map/ppermute | solution.py:62
  341.4 5.2 %collective-permute-start.17 = (f32[4,1024]{1,0:T(4,128)S(1)}, f32[4,1024]{1,0:T(4,128)S(1)}, u32[]{:S(2)}, u32[]{:S(2)}) collective-permute-start(f32[4,1024]{1,0:T(4,128)S(1)} %bitcast.45), channel_id=1, source_target_pairs={{0,16},{4,20},{8,24},{12,28},{16,0},{20,4},{24,8},{28,12},{1,17},{... | collective-permute-start | bytes 49160 | tf_op jit(solution)/shard_map/ppermute | solution.py:117
  346.6 2.9 collective-permute-start.18
  349.5 22.6 %collective-permute-start.19 = (f32[1,1024]{1,0:T(1,128)S(1)}, f32[1,1024]{1,0:T(1,128)S(1)}, u32[]{:S(2)}, u32[]{:S(2)}) collective-permute-start(f32[1,1024]{1,0:T(1,128)S(1)} %broadcast_select_fusion.3), channel_id=1, source_target_pairs={{0,4},{4,0},{8,12},{12,8},{16,20},{20,16},{24,28},{28,24},{1,5},{5... | collective-permute-start | bytes 12296 | tf_op jit(solution)/shard_map/ppermute | solution.py:117
  375.0 24.4 %collective-permute-start.22 = (bf16[512,1024]{1,0:T(8,128)(2,1)}, bf16[512,1024]{1,0:T(8,128)(2,1)}, u32[]{:S(2)}, u32[]{:S(2)}) collective-permute-start(bf16[512,1024]{1,0:T(8,128)(2,1)} %add_convert_fusion.1), channel_id=1, source_target_pairs={{0,1},{1,2},{2,3},{3,0},{4,5},{5,6},{6,7},{7,4},{8,9},{9,10},{10,1... | collective-permute-start | bytes 3145736 | tf_op jit(solution)/shard_map/ppermute | solution.py:62
  377.1 27.5 %copy-start.3 = (bf16[2048,256]{1,0:T(8,128)(2,1)S(1)}, bf16[2048,256]{1,0:T(8,128)(2,1)}, u32[]{:S(2)}) copy-start(bf16[2048,256]{1,0:T(8,128)(2,1)} %param.15) | copy-start | bytes 3145732
  377.1 27.5 %copy-start.29 = (f32[256]{0:T(256)S(1)}, f32[256]{0:T(256)}, u32[]{:S(2)}) copy-start(f32[256]{0:T(256)} %param.28) | copy-start | bytes 3076
  377.2 22.2 %collective-permute-start.21 = (f32[3072]{0:T(1024)S(1)}, f32[3072]{0:T(1024)S(1)}, u32[]{:S(2)}, u32[]{:S(2)}) collective-permute-start(f32[3072]{0:T(1024)S(1)} %pad_maximum_fusion.1), channel_id=1, source_target_pairs={{0,1},{1,0},{2,3},{3,2},{4,5},{5,4},{6,7},{7,6},{8,9},{9,8},{10,11... | collective-permute-start | bytes 36872 | tf_op jit(solution)/shard_map/ppermute | solution.py:108
  402.3 29.4 %collective-permute-start.24 = (bf16[512,1024]{1,0:T(8,128)(2,1)}, bf16[512,1024]{1,0:T(8,128)(2,1)}, u32[]{:S(2)}, u32[]{:S(2)}) collective-permute-start(bf16[512,1024]{1,0:T(8,128)(2,1)} %add_convert_fusion), channel_id=1, source_target_pairs={{0,1},{1,2},{2,3},{3,0},{4,5},{5,6},{6,7},{7,4},{8,9},{9,10},{10,1... | collective-permute-start | bytes 3145736 | tf_op jit(solution)/shard_map/ppermute | solution.py:62
  404.6 25.3 %collective-permute-start.23 = (f32[3072]{0:T(1024)S(1)}, f32[3072]{0:T(1024)S(1)}, u32[]{:S(2)}, u32[]{:S(2)}) collective-permute-start(f32[3072]{0:T(1024)S(1)} %fusion.11), channel_id=1, source_target_pairs={{0,2},{1,3},{2,0},{3,1},{4,6},{5,7},{6,4},{7,5},{8,10},{9,11},{10,... | collective-permute-start | bytes 36872 | tf_op jit(solution)/shard_map/ppermute | solution.py:108
  (34 other events, 377.4 us)
Sparse Core Ops, SparseCore 0:
  9.9 56.5 all-gather.2
  68.3 55.9 all-gather.4
  263.3 83.5 reduce-scatter.2
  350.6 71.3 reduce-scatter.4
